TPU v7x, 512 devices: a whole 4x8x8 slice. The times are simulated.
512 devices in a mesh: seq: 32 (over z, x), chan: 16 (over y, core).
Axes of the slice: x: 4, y: 8, z: 8, core: 2. Of those that a mesh axis runs over, the one named last changes fastest.
Arguments:
- streams: bfloat16 [3, 16384, 4096], P(None, 'seq', 'chan'), may hold values from -6 to 6
- short_weight: float32 [3, 3, 4096], P(None, None, 'chan'), may hold values from -3 to 3
- short_bias: float32 [3, 4096], P(None, 'chan'), may hold values from -3 to 3
- spectrum: bfloat16 [2, 2, 16384, 4096], P(None, None, ('chan', 'seq')), may hold values from -6 to 6
- skip_gain: float32 [4096], P('chan'), may hold values from -4 to 4
Outputs:
- mixed: bfloat16 [16384, 4096], P('seq', 'chan')
All inputs are finite; a program needn't handle non-finite values.
Results may differ from a plain program's by a relative error of at most 0.01.
Values may be sent and summed in bfloat16 or wider, within the bound.
No kernel may reach another device: no remote copies, remote signals or barrier semaphores. Data moves between devices by JAX's collectives and lax.ppermute only.
A program may use at most 64 MiB of HBM per device.

v0:
```python
import functools

import jax
import jax.numpy as jnp
import numpy as np
from jax import lax
from jax.experimental import pallas as pl
from jax.experimental.pallas import tpu as pltpu
from jax.sharding import PartitionSpec as P

F32 = jnp.float32
BF16 = jnp.bfloat16
VMEM_LIMIT = 56 * 1024 * 1024


def dot_t(lhs, rhs):
    return lax.dot_general(lhs, rhs, (((1,), (1,)), ((), ())), preferred_element_type=F32)


def dot(lhs, rhs):
    return jnp.dot(lhs, rhs, preferred_element_type=F32)


class Plan:
    def __init__(self, seq, chans, tokens, channels):
        self.seq = seq
        self.own = channels // (seq * chans)
        self.span = tokens // seq
        self.total = 2 * tokens
        self.lows = 2 * seq
        self.rows = self.own * self.lows

    def low_order(self):
        q = np.arange(self.lows)
        half = self.lows // 2
        return 2 * (q % half) + q // half

    def first_table(self):
        low = self.low_order()
        s = np.arange(self.seq)
        angle = 2.0 * np.pi * ((low[:, None] * s[None, :]) % self.lows) / self.lows
        eye = np.eye(self.own)
        parts = np.stack([np.cos(angle), np.sin(angle)])
        full = np.einsum("pqs,cd->pcqsd", parts, eye)
        return full.reshape(2 * self.rows, self.seq * self.own)

    def last_table(self):
        low = self.low_order()
        s = np.arange(self.seq)
        angle = 2.0 * np.pi * ((low[:, None] * s[None, :]) % self.lows) / self.lows
        eye = np.eye(self.own)
        parts = np.stack([np.cos(angle), -np.sin(angle)])
        full = np.einsum("pqs,cd->sdpcq", parts, eye)
        return full.reshape(self.seq * self.own, 2 * self.rows)

    def big_table(self):
        d = np.arange(self.span)
        angle = 2.0 * np.pi * ((d[:, None] * d[None, :]) % self.span) / self.span
        c, s = np.cos(angle), np.sin(angle)
        return np.block([[c, -s], [s, c]])

    def twiddle(self):
        low = self.low_order()
        a = np.arange(self.span)
        angle = 2.0 * np.pi * ((low[:, None] * a[None, :]) % self.total) / self.total
        return np.stack([np.cos(angle), np.sin(angle)])


def spectrum_kernel(spec_ref, eye_ref, out_ref):
    eye = eye_ref[...]
    rows = [spec_ref[r, i] for i in range(2) for r in range(2)]
    block = jnp.concatenate(rows, axis=0)
    width = eye.shape[0]
    for j in range(block.shape[1] // width):
        piece = block[:, j * width : (j + 1) * width]
        out_ref[j * width : (j + 1) * width, :] = dot_t(eye, piece).astype(BF16)


def transpose_spectrum(spectrum, eye, per_step):
    rows = 4 * spectrum.shape[2]
    chans = spectrum.shape[3]
    return pl.pallas_call(
        spectrum_kernel,
        grid=(chans // per_step,),
        in_specs=[
            pl.BlockSpec((2, 2, spectrum.shape[2], per_step), lambda g: (0, 0, 0, g)),
            pl.BlockSpec(eye.shape, lambda g: (0, 0)),
        ],
        out_specs=pl.BlockSpec((per_step, rows), lambda g: (g, 0)),
        out_shape=jax.ShapeDtypeStruct((chans, rows), BF16),
        cost_estimate=pl.CostEstimate(
            flops=2 * rows * chans * eye.shape[0], bytes_accessed=4 * rows * chans, transcendentals=0
        ),
        name="transpose_spectrum",
    )(spectrum, eye)


def conv_kernel(streams_ref, halo_ref, weight_ref, bias_ref, eye_ref, u_ref, ut_ref, gate_ref):
    length = streams_ref.shape[1]
    row = lax.broadcasted_iota(jnp.int32, (length, streams_ref.shape[2]), 0)

    def short(k):
        now = streams_ref[k].astype(F32)
        halo = halo_ref[k].astype(F32)
        one = jnp.where(row == 0, halo[1:2, :], pltpu.roll(now, 1, 0))
        two = pltpu.roll(now, 2, 0)
        two = jnp.where(row == 0, halo[0:1, :], jnp.where(row == 1, halo[1:2, :], two))
        return (
            weight_ref[0, k : k + 1, :] * now
            + weight_ref[1, k : k + 1, :] * one
            + weight_ref[2, k : k + 1, :] * two
            + bias_ref[k : k + 1, :]
        )

    u = (short(1) * short(2)).astype(BF16)
    u_ref[...] = u
    ut_ref[...] = dot_t(eye_ref[...], u).astype(BF16)
    gate_ref[...] = short(0)


def short_conv(streams, halo, weight, bias, eye):
    _, length, chans = streams.shape
    return pl.pallas_call(
        conv_kernel,
        out_shape=(
            jax.ShapeDtypeStruct((length, chans), BF16),
            jax.ShapeDtypeStruct((chans, length), BF16),
            jax.ShapeDtypeStruct((length, chans), F32),
        ),
        cost_estimate=pl.CostEstimate(
            flops=2 * length * chans * chans, bytes_accessed=14 * length * chans, transcendentals=0
        ),
        compiler_params=pltpu.CompilerParams(vmem_limit_bytes=VMEM_LIMIT),
        name="short_conv",
    )(streams, halo, weight, bias, eye)


def filter_kernel(recv_ref, out_ref, wide_ref):
    depth, own, lanes = recv_ref.shape
    half = lanes // 2
    wide_ref[...] = recv_ref[...].astype(F32)
    first = lax.broadcasted_iota(jnp.int32, (depth, lanes), 1) < half
    for pair in range(own // 2):
        even = wide_ref[:, 2 * pair, :]
        odd = wide_ref[:, 2 * pair + 1, :]
        span = slice(pair * lanes, (pair + 1) * lanes)
        out_ref[:depth, span] = jnp.where(first, even, pltpu.roll(odd, half, 1))
        out_ref[depth:, span] = jnp.where(first, pltpu.roll(even, half, 1), odd)


def arrange_filter(recv):
    depth, own, lanes = recv.shape
    return pl.pallas_call(
        filter_kernel,
        out_shape=jax.ShapeDtypeStruct((2 * depth, own * lanes // 2), F32),
        scratch_shapes=[pltpu.VMEM((depth, own, lanes), F32)],
        cost_estimate=pl.CostEstimate(
            flops=4 * depth * own * lanes, bytes_accessed=6 * depth * own * lanes, transcendentals=0
        ),
        compiler_params=pltpu.CompilerParams(vmem_limit_bytes=VMEM_LIMIT),
        name="arrange_filter",
    )(recv)


def transform_kernel(plan, u_ref, filt_ref, first_ref, big_ref, tw_ref, twt_ref, last_ref, y_ref, g_ref, yf_ref, b_ref):
    span, lows, own, rows = plan.span, plan.lows, plan.own, plan.rows
    u = u_ref[...]
    for c in range(own):
        re = dot(first_ref[c * lows : (c + 1) * lows, :], u)
        im = dot(first_ref[rows + c * lows : rows + (c + 1) * lows, :], u)
        g_ref[c * lows : (c + 1) * lows, :span] = (re * tw_ref[0] - im * tw_ref[1]).astype(BF16)
        g_ref[c * lows : (c + 1) * lows, span:] = (re * tw_ref[1] + im * tw_ref[0]).astype(BF16)
    lanes = 2 * lows
    block = 2 * lanes
    for j in range(rows // block):
        sl = slice(j * block, (j + 1) * block)
        xr = dot_t(big_ref[:span, :], g_ref[sl, :])
        xi = dot_t(big_ref[span:, :], g_ref[sl, :])
        hr = filt_ref[:span, sl]
        hi = filt_ref[span:, sl]
        yf_ref[:span, sl] = (hr * xr + hi * xi).astype(BF16)
        yf_ref[span:, sl] = (hi * xr - hr * xi).astype(BF16)
        br = dot(big_ref[:span, :], yf_ref[:, sl])
        bi = dot(big_ref[span:, :], yf_ref[:, sl])
        b_ref[:, sl] = (br * twt_ref[0] - bi * twt_ref[1]).astype(BF16)
        b_ref[:, rows + j * block : rows + (j + 1) * block] = (
            br * twt_ref[1] + bi * twt_ref[0]
        ).astype(BF16)
    y_ref[...] = (dot_t(last_ref[...], b_ref[...]) * (1.0 / plan.total)).astype(BF16)


def transform(plan, u, filt, tables):
    rows, span = plan.rows, plan.span
    macs = 2 * (2 * rows * u.shape[0] * span + 4 * span * span * rows)
    return pl.pallas_call(
        functools.partial(transform_kernel, plan),
        out_shape=jax.ShapeDtypeStruct(u.shape, BF16),
        scratch_shapes=[
            pltpu.VMEM((rows, 2 * span), BF16),
            pltpu.VMEM((2 * span, rows), BF16),
            pltpu.VMEM((span, 2 * rows), BF16),
        ],
        cost_estimate=pl.CostEstimate(flops=2 * macs, bytes_accessed=6 * 1024 * 1024, transcendentals=0),
        compiler_params=pltpu.CompilerParams(vmem_limit_bytes=VMEM_LIMIT),
        name="transform",
    )(u, filt, *tables)


def final_kernel(y_ref, u_ref, gate_ref, skip_ref, out_ref):
    conv = y_ref[...].astype(F32).T
    u = u_ref[...].astype(F32)
    out_ref[...] = ((conv + u * skip_ref[...]) * gate_ref[...]).astype(BF16)


def finish(y, u, gate, skip):
    length, chans = u.shape
    return pl.pallas_call(
        final_kernel,
        out_shape=jax.ShapeDtypeStruct((length, chans), BF16),
        cost_estimate=pl.CostEstimate(
            flops=4 * length * chans, bytes_accessed=10 * length * chans, transcendentals=0
        ),
        compiler_params=pltpu.CompilerParams(vmem_limit_bytes=VMEM_LIMIT),
        name="finish",
    )(y, u, gate, skip)


def exchange(values, axes):
    return lax.all_to_all(values, axes, split_axis=0, concat_axis=0, tiled=True)


def on_device(plan, tables, eye, streams, short_weight, short_bias, spectrum, skip_gain):
    seq = plan.seq
    own = plan.own
    length = streams.shape[1]
    chans = streams.shape[2]
    parts = 4 * spectrum.shape[2]
    sent = transpose_spectrum(spectrum, eye, spectrum.shape[3] // 4)
    recv = exchange(sent.reshape(-1, own, parts), ("chan", "seq"))
    filt = arrange_filter(recv)

    route = [(i, i + 1) for i in range(seq - 1)]
    halo = lax.ppermute(streams[:, length - 2 :, :], "seq", route)
    u, ut, gate = short_conv(streams, halo, short_weight, short_bias, eye)
    mine = exchange(ut.reshape(seq, own, length), "seq").reshape(seq * own, length)
    y = transform(plan, mine, filt, tables)
    back = exchange(y.reshape(seq, own, length), "seq").reshape(chans, length)
    return finish(back, u, gate, skip_gain[None, :])


def solution(mesh):
    seq = mesh.shape["seq"]
    chans = mesh.shape["chan"]
    plan = Plan(seq, chans, 16384, 4096)
    eye = jnp.asarray(np.eye(256), BF16)
    tw = plan.twiddle()
    twt = np.tile(tw.transpose(0, 2, 1), (1, 1, 4))
    tables = (
        jnp.asarray(plan.first_table(), BF16),
        jnp.asarray(plan.big_table(), BF16),
        jnp.asarray(tw, F32),
        jnp.asarray(twt, F32),
        jnp.asarray(plan.last_table(), BF16),
    )
    placed = (
        P(None, "seq", "chan"),
        P(None, None, "chan"),
        P(None, "chan"),
        P(None, None, ("chan", "seq"), None),
        P("chan"),
    )
    return jax.shard_map(
        functools.partial(on_device, plan, tables, eye),
        mesh=mesh,
        in_specs=placed,
        out_specs=P("seq", "chan"),
        check_vma=False,
    )
```

profile of v0, /device:TPU:8, one launch (start us, length us, event | category | flops | bytes accessed | tf_op | source)
XLA Modules:
  0.0 101.9 jit_solution(7880857778881397840)
XLA Ops:
  0.0 4.0 %transpose_spectrum.1 = bf16[4096,128]{1,0:T(8,128)(2,1)} custom-call(bf16[2,2,32,4096]{3,2,1,0:T(8,128)(2,1)} %spec_ref.1, bf16[256,256]{1,0:T(8,128)(2,1)} %constant.12.clone.eye_ref), custom_call_target="tpu_custom_call" | custom-call | flops 268435456 | bytes 2097152 | tf_op jit(solution)/shard_map/transpose_spectrum/pallas_call | solution.py:82
  4.0 21.1 %all-to-all-start.1 = ((bf16[512,8,128]{2,1,0:T(8,128)(2,1)}), bf16[512,8,128]{2,1,0:T(8,128)(2,1)S(1)}, u32[]{:S(2)}, u32[]{:S(2)}) async-start(bf16[512,8,128]{2,1,0:T(8,128)(2,1)} %bitcast.6), calls=%async_computation.1 | async-start | bytes 2097152 | tf_op jit(solution)/shard_map/all_to_all | solution.py:229
  25.1 0.7 slice.3
  25.8 3.4 %collective-permute-start = (bf16[3,2,256]{2,1,0:T(2,128)(2,1)S(1)}, bf16[3,2,256]{2,1,0:T(2,128)(2,1)S(1)}, u32[]{:S(2)}, u32[]{:S(2)}) collective-permute-start(bf16[3,2,256]{2,1,0:T(2,128)(2,1)S(1)} %slice.3), channel_id=1, source_target_pairs={{0,16},{16,32},{32,48},{48,64},{64,80},{80,96},{96,112},{112,128},... | collective-permute-start | bytes 9224 | tf_op jit(solution)/shard_map/ppermute | solution.py:243
  29.1 1.3 %collective-permute-done.halo_ref = bf16[3,2,256]{2,1,0:T(2,128)(2,1)S(1)} collective-permute-done((bf16[3,2,256]{2,1,0:T(2,128)(2,1)S(1)}, bf16[3,2,256]{2,1,0:T(2,128)(2,1)S(1)}, u32[]{:S(2)}, u32[]{:S(2)}) %collective-permute-start) | collective-permute-done | bytes 3104 | tf_op jit(solution)/shard_map/ppermute | solution.py:243
  30.5 0.0 copy-start.2
  30.5 0.6 copy-done.2
  31.0 3.0 %short_conv.1 = (bf16[512,256]{1,0:T(8,128)(2,1)}, bf16[256,512]{1,0:T(8,128)(2,1)}, f32[512,256]{1,0:T(8,128)}) custom-call(bf16[3,512,256]{2,1,0:T(8,128)(2,1)} %streams_ref.1, bf16[3,2,256]{2,1,0:T(2,128)(2,1)} %copy-done.2, f32[3,3,256]{2,1,0:T(4,128)} %weight_ref.1, f32[3,256]{1,0:T(4,128)} %bias_ref.1, bf16[256,256]{1,0:T(8,128)(2,1)} %constant.12.clone.eye_ref), custom_call_target="tpu_custom_call" | custom-call | flops 67108864 | bytes 1835008 | tf_op jit(solution)/shard_map/short_conv/pallas_call | solution.py:123
  34.1 23.4 %all-to-all-done.1.recv_ref = bf16[512,8,128]{2,1,0:T(8,128)(2,1)S(1)} async-done(((bf16[512,8,128]{2,1,0:T(8,128)(2,1)}), bf16[512,8,128]{2,1,0:T(8,128)(2,1)S(1)}, u32[]{:S(2)}, u32[]{:S(2)}) %all-to-all-start.1) | async-done | bytes 1048608 | tf_op jit(solution)/shard_map/all_to_all | solution.py:229
  57.5 0.0 copy-start
  57.5 5.7 %all-to-all-start = ((bf16[32,8,512]{2,1,0:T(8,128)(2,1)}), bf16[32,8,512]{2,1,0:T(8,128)(2,1)S(1)}, u32[]{:S(2)}, u32[]{:S(2)}) async-start(bf16[32,8,512]{2,1,0:T(8,128)(2,1)} %bitcast.8), calls=%async_computation | async-start | bytes 524288 | tf_op jit(solution)/shard_map/all_to_all | solution.py:229
  63.2 0.0 copy-done
  63.2 3.9 %arrange_filter.1.filt_ref = f32[1024,512]{1,0:T(8,128)} custom-call(bf16[512,8,128]{2,1,0:T(8,128)(2,1)} %copy-done), custom_call_target="tpu_custom_call" | custom-call | flops 2097152 | bytes 3145728 | tf_op jit(solution)/shard_map/arrange_filter/pallas_call | solution.py:153
  67.1 8.5 %all-to-all-done = bf16[32,8,512]{2,1,0:T(8,128)(2,1)S(1)} async-done(((bf16[32,8,512]{2,1,0:T(8,128)(2,1)}), bf16[32,8,512]{2,1,0:T(8,128)(2,1)S(1)}, u32[]{:S(2)}, u32[]{:S(2)}) %all-to-all-start) | async-done | bytes 262176 | tf_op jit(solution)/shard_map/all_to_all | solution.py:229
  75.5 0.0 copy-start.1
  75.5 0.7 copy-done.1
  76.2 7.3 %transform.1 = bf16[256,512]{1,0:T(8,128)(2,1)} custom-call(bf16[256,512]{1,0:T(8,128)(2,1)} %bitcast.9, f32[1024,512]{1,0:T(8,128)} %arrange_filter.1.filt_ref, bf16[1024,256]{1,0:T(8,128)(2,1)} %constant.13.clone.first_ref, bf16[1024,1024]{1,0:T(8,128)(2,1)} %constant.14.clone.big_ref, f32[2,64,512]{2,1,0:T(8,128)} %constant.15.clone.tw_ref, ...), custom_call_target="tpu_custom_call" | custom-call | flops 2684354560 | bytes 6291456 | tf_op jit(solution)/shard_map/transform/pallas_call | solution.py:195
  83.6 16.3 %all_to_all.15 = bf16[32,8,512]{2,1,0:T(8,128)(2,1)} all-to-all(bf16[32,8,512]{2,1,0:T(8,128)(2,1)} %bitcast.10), channel_id=1, replica_groups=mesh['seq'=32,'chan'=16] {'seq'}, dimensions={0} | all-to-all | bytes 524288 | tf_op jit(solution)/shard_map/all_to_all | solution.py:229
  99.8 2.1 %finish.1 = bf16[512,256]{1,0:T(8,128)(2,1)} custom-call(bf16[256,512]{1,0:T(8,128)(2,1)} %bitcast.7, bf16[512,256]{1,0:T(8,128)(2,1)} %get-tuple-element.9.u_ref, f32[512,256]{1,0:T(8,128)} %get-tuple-element.10.gate_ref, f32[1,256]{1,0:T(1,128)} %bitcast.11), custom_call_target="tpu_custom_call" | custom-call | flops 524288 | bytes 1310720 | tf_op jit(solution)/shard_map/finish/pallas_call | solution.py:217
Async XLA Ops:
  4.0 53.5 %all-to-all-start.1 = ((bf16[512,8,128]{2,1,0:T(8,128)(2,1)}), bf16[512,8,128]{2,1,0:T(8,128)(2,1)S(1)}, u32[]{:S(2)}, u32[]{:S(2)}) async-start(bf16[512,8,128]{2,1,0:T(8,128)(2,1)} %bitcast.6), calls=%async_computation.1 | async-start | bytes 2097152 | tf_op jit(solution)/shard_map/all_to_all | solution.py:229
  25.8 4.7 %collective-permute-start = (bf16[3,2,256]{2,1,0:T(2,128)(2,1)S(1)}, bf16[3,2,256]{2,1,0:T(2,128)(2,1)S(1)}, u32[]{:S(2)}, u32[]{:S(2)}) collective-permute-start(bf16[3,2,256]{2,1,0:T(2,128)(2,1)S(1)} %slice.3), channel_id=1, source_target_pairs={{0,16},{16,32},{32,48},{48,64},{64,80},{80,96},{96,112},{112,128},... | collective-permute-start | bytes 9224 | tf_op jit(solution)/shard_map/ppermute | solution.py:243
  30.5 0.6 copy-start.2
  57.5 5.7 %copy-start = (bf16[512,8,128]{2,1,0:T(8,128)(2,1)}, bf16[512,8,128]{2,1,0:T(8,128)(2,1)S(1)}, u32[]{:S(2)}) copy-start(bf16[512,8,128]{2,1,0:T(8,128)(2,1)S(1)} %all-to-all-done.1.recv_ref) | copy-start | bytes 3145732
  57.5 18.0 %all-to-all-start = ((bf16[32,8,512]{2,1,0:T(8,128)(2,1)}), bf16[32,8,512]{2,1,0:T(8,128)(2,1)S(1)}, u32[]{:S(2)}, u32[]{:S(2)}) async-start(bf16[32,8,512]{2,1,0:T(8,128)(2,1)} %bitcast.8), calls=%async_computation | async-start | bytes 524288 | tf_op jit(solution)/shard_map/all_to_all | solution.py:229
  75.5 0.7 copy-start.1
where the time goes:
time: 102 us
  waiting for transfers between devices  33.2 us (33%)
  starting transfers between devices  30.1 us (30%)
  Pallas kernels  20.2 us (20%)
  blocking collectives  16.3 us (16%)
  local copies, waits for them, and re-layouts  2 us (2%)
    all_to_all x2, waiting for transfers between devices, exchange(): return lax.all_to_all(values, axes, split_axis=0, concat_axis=0, tiled=True)  31.9 us
    all_to_all x2, starting transfers between devices, exchange(): return lax.all_to_all(values, axes, split_axis=0, concat_axis=0, tiled=True)  26.8 us
    all_to_all x1, blocking collectives, exchange(): return lax.all_to_all(values, axes, split_axis=0, concat_axis=0, tiled=True)  16.3 us
    pallas_call x1, Pallas kernels, transform(): pl.pallas_call(functools.partial(transform_kernel, plan), out_shape=jax.S...  7.31 us
    pallas_call x1, Pallas kernels, transpose_spectrum(): pl.pallas_call(spectrum_kernel, grid=(chans // per_step,), in_specs=[pl.B...  3.95 us
    pallas_call x1, Pallas kernels, arrange_filter(): pl.pallas_call(filter_kernel, out_shape=jax.ShapeDtypeStruct((2 * depth,...  3.89 us
    ppermute x1, starting transfers between devices, on_device(): halo = lax.ppermute(streams[:, length - 2:, :], 'seq', route)  3.36 us
    pallas_call x1, Pallas kernels, short_conv(): pl.pallas_call(conv_kernel, out_shape=(jax.ShapeDtypeStruct((length, chan...  3.04 us
  transfers between devices with their start and end apart: 3, of which 3 were waited for; matrix products, arithmetic and copies ran while one was open for 1% of the time, Pallas kernels for 7%

commit v1 on v0

v1 whole, which is shorter than its diff:
```python
import functools

import jax
import jax.numpy as jnp
import numpy as np
from jax import lax
from jax.experimental import pallas as pl
from jax.experimental.pallas import tpu as pltpu
from jax.sharding import PartitionSpec as P

F32 = jnp.float32
BF16 = jnp.bfloat16
VMEM_LIMIT = 20 * 1024 * 1024
VMEM_WHOLE = 56 * 1024 * 1024


def dot_t(lhs, rhs):
    return lax.dot_general(lhs, rhs, (((1,), (1,)), ((), ())), preferred_element_type=F32)


def dot(lhs, rhs):
    return jnp.dot(lhs, rhs, preferred_element_type=F32)


class Plan:
    def __init__(self, seq, chans, tokens, channels, groups):
        self.seq = seq
        self.own = channels // (seq * chans)
        self.span = tokens // seq
        self.total = 2 * tokens
        self.groups = groups
        self.members = self.own // groups
        self.spare = 16
        self.base = self.members * seq
        self.rows = self.base + self.spare
        q = np.arange(seq)
        half = seq // 2
        self.lows = 2 * (q % half) + q // half

    def stage_table(self):
        out = np.zeros((self.groups, 2, self.rows, self.seq, self.own))
        s = np.arange(self.seq)
        for ch in range(self.own):
            g, c = divmod(ch, self.members)
            at = [c * self.seq + q for q in range(self.seq)] + [self.base + c]
            low = np.append(self.lows, self.seq)
            angle = 2.0 * np.pi * ((low[:, None] * s) % (2 * self.seq)) / (2 * self.seq)
            out[g, 0, at, :, ch] = np.cos(angle)
            out[g, 1, at, :, ch] = np.sin(angle)
        return out

    def first_table(self):
        return self.stage_table().reshape(-1, self.seq * self.own)

    def last_table(self):
        table = self.stage_table() / self.total
        table[:, 1] *= -1.0
        return table.reshape(-1, self.seq * self.own).T

    def big_table(self):
        d = np.arange(self.span)
        angle = 2.0 * np.pi * ((d[:, None] * d[None, :]) % self.span) / self.span
        return np.concatenate([np.cos(angle), np.sin(angle)])

    def twiddle(self):
        low = np.append(self.lows, [self.seq] * self.spare)
        a = np.arange(self.span)
        angle = 2.0 * np.pi * ((low[:, None] * a[None, :]) % self.total) / self.total
        return np.stack([np.cos(angle), np.sin(angle)])

    def fold_table(self):
        half = self.seq
        lanes = 4 * self.seq
        out = np.zeros((2 * self.seq + 8, 2 * lanes))

        def lane(part, low):
            return part * 2 * half + (low % 2) * half + low // 2

        for q, low in enumerate(self.lows):
            for part in range(2):
                out[part * self.seq + q, lane(part, low)] = 1.0
                if low:
                    out[part * self.seq + q, lanes + lane(part, 2 * self.seq - low)] = 1.0 - 2.0 * part
        for part in range(2):
            out[2 * self.seq + part, lane(part, self.seq)] = 1.0
        return out


def spectrum_kernel(spec_ref, out_ref, held_ref, turned_ref, in_sems, out_sems):
    steps, _, _, _, wide = held_ref.shape
    fetches = [
        pltpu.make_async_copy(
            spec_ref.at[:, :, :, pl.ds(j * wide, wide)], held_ref.at[j], in_sems.at[j]
        )
        for j in range(steps)
    ]
    stores = [
        pltpu.make_async_copy(
            turned_ref.at[j], out_ref.at[pl.ds(j * wide, wide), :], out_sems.at[j]
        )
        for j in range(steps)
    ]
    for fetch in fetches:
        fetch.start()
    for j in range(steps):
        fetches[j].wait()
        rows = [held_ref[j, r, i] for i in range(2) for r in range(2)]
        turned_ref[j] = jnp.concatenate(rows, axis=0).T
        stores[j].start()
    for store in stores:
        store.wait()


def transpose_spectrum(spectrum, steps):
    rows = 4 * spectrum.shape[2]
    chans = spectrum.shape[3]
    return pl.pallas_call(
        spectrum_kernel,
        in_specs=[pl.BlockSpec(memory_space=pl.ANY)],
        out_specs=pl.BlockSpec(memory_space=pl.ANY),
        out_shape=jax.ShapeDtypeStruct((chans, rows), BF16),
        scratch_shapes=[
            pltpu.VMEM((steps, 2, 2, spectrum.shape[2], chans // steps), BF16),
            pltpu.VMEM((steps, chans // steps, rows), BF16),
            pltpu.SemaphoreType.DMA((steps,)),
            pltpu.SemaphoreType.DMA((steps,)),
        ],
        cost_estimate=pl.CostEstimate(
            flops=rows * chans, bytes_accessed=4 * rows * chans, transcendentals=0
        ),
        compiler_params=pltpu.CompilerParams(vmem_limit_bytes=VMEM_WHOLE),
        name="transpose_spectrum",
    )(spectrum)


def short(stream, halo, weight, bias):
    row = lax.broadcasted_iota(jnp.int32, stream.shape, 0)
    now = stream.astype(F32)
    before = halo.astype(F32)
    one = jnp.where(row == 0, before[1:2, :], pltpu.roll(now, 1, 0))
    two = pltpu.roll(now, 2, 0)
    two = jnp.where(row == 0, before[0:1, :], jnp.where(row == 1, before[1:2, :], two))
    return weight[0:1] * now + weight[1:2] * one + weight[2:3] * two + bias


def conv_kernel(streams_ref, halo_ref, weight_ref, bias_ref, skip_ref, ut_ref, direct_ref, gate_ref):
    def stream(k):
        return short(streams_ref[k], halo_ref[k], weight_ref[:, k, :], bias_ref[k : k + 1, :])

    u = (stream(1) * stream(2)).astype(BF16)
    ut_ref[...] = u.T
    direct_ref[...] = u.astype(F32) * skip_ref[...]
    gate_ref[...] = stream(0)


def short_conv(streams, halo, weight, bias, skip):
    _, length, chans = streams.shape
    return pl.pallas_call(
        conv_kernel,
        out_shape=(
            jax.ShapeDtypeStruct((chans, length), BF16),
            jax.ShapeDtypeStruct((length, chans), F32),
            jax.ShapeDtypeStruct((length, chans), F32),
        ),
        cost_estimate=pl.CostEstimate(
            flops=20 * length * chans, bytes_accessed=16 * length * chans, transcendentals=0
        ),
        compiler_params=pltpu.CompilerParams(vmem_limit_bytes=VMEM_LIMIT),
        name="short_conv",
    )(streams, halo, weight, bias, skip)


def filter_kernel(plan, recv_ref, fold_ref, out_ref, wide_ref):
    depth = recv_ref.shape[0]
    seq, rows, base = plan.seq, plan.rows, plan.base
    wide_ref[...] = recv_ref[...].astype(F32)
    row = lax.broadcasted_iota(jnp.int32, (depth, depth), 0)
    column = lax.broadcasted_iota(jnp.int32, (depth, depth), 1)
    reverse = jnp.where(row + column == depth - 1, 1.0, 0.0).astype(BF16)
    for g in range(plan.groups):
        for part in range(2):
            first = (2 * g + part) * rows + base
            out_ref[first : first + plan.spare, :] = jnp.zeros((plan.spare, depth), BF16)
    for ch in range(plan.own):
        g, c = divmod(ch, plan.members)
        turned = wide_ref[:, ch, :].astype(BF16).T
        back = dot(turned, reverse).astype(BF16)
        folded = dot(fold_ref[...], jnp.concatenate([turned, back], axis=0)).astype(BF16)
        for part in range(2):
            first = (2 * g + part) * rows
            out_ref[first + c * seq : first + (c + 1) * seq, :] = folded[part * seq : (part + 1) * seq]
            at = 2 * seq + part
            out_ref[first + base + c : first + base + c + 1, :] = folded[at : at + 1]


def arrange_filter(plan, recv, fold):
    depth, own, lanes = recv.shape
    return pl.pallas_call(
        functools.partial(filter_kernel, plan),
        out_shape=jax.ShapeDtypeStruct((2 * plan.groups * plan.rows, depth), BF16),
        scratch_shapes=[pltpu.VMEM((depth, own, lanes), F32)],
        cost_estimate=pl.CostEstimate(
            flops=2 * depth * own * lanes * depth, bytes_accessed=6 * depth * own * lanes, transcendentals=0
        ),
        compiler_params=pltpu.CompilerParams(vmem_limit_bytes=VMEM_LIMIT),
        name="arrange_filter",
    )(recv, fold)


def transform_kernel(plan, *refs):
    count = 6
    sources, y_ref, held = refs[:count], refs[count], refs[count + 1 : 2 * count + 1]
    left_ref, b_ref, sems = refs[2 * count + 1 :]
    fetches = [pltpu.make_async_copy(s, h, sems.at[j]) for j, (s, h) in enumerate(zip(sources, held))]
    for fetch in fetches:
        fetch.start()
    u_ref, first_ref, tw_ref, big_ref, filt_ref, last_ref = held
    seq, rows, base, span = plan.seq, plan.rows, plan.base, plan.span
    fetches[0].wait()
    fetches[1].wait()
    u = u_ref[...]
    stages = [
        dot(first_ref[2 * g * rows : 2 * (g + 1) * rows, :], u) for g in range(plan.groups)
    ]
    fetches[2].wait()

    def turn(re, im):
        parts = []
        for at in list(range(0, base, seq)) + [base]:
            size = seq if at < base else plan.spare
            first = 0 if at < base else seq
            c = tw_ref[0, first : first + size, :]
            s = tw_ref[1, first : first + size, :]
            r, i = re[at : at + size], im[at : at + size]
            parts.append((r * c - i * s, r * s + i * c))
        return [jnp.concatenate(p, axis=0).astype(BF16) for p in zip(*parts)]

    def multiply(re, im):
        left_ref[:rows, :span] = re
        left_ref[:rows, span:] = -im
        left_ref[rows:, :span] = im
        left_ref[rows:, span:] = re
        out = dot(left_ref[...], big_ref[...])
        return out[:rows], out[rows:]

    turned = [turn(stage[:rows], stage[rows:]) for stage in stages]
    fetches[3].wait()
    fetches[4].wait()
    for g in range(plan.groups):
        lo, mid, hi = (2 * g) * rows, (2 * g + 1) * rows, (2 * g + 2) * rows
        xr, xi = multiply(*turned[g])
        hr = filt_ref[lo:mid, :].astype(F32)
        h_im = filt_ref[mid:hi, :].astype(F32)
        yr = (hr * xr + h_im * xi).astype(BF16)
        yi = (h_im * xr - hr * xi).astype(BF16)
        br, bi = turn(*multiply(yr, yi))
        b_ref[lo:mid, :] = br
        b_ref[mid:hi, :] = bi
    fetches[5].wait()
    y_ref[...] = dot(last_ref[...], b_ref[...]).astype(BF16)


def transform(plan, u, filt, tables):
    rows, span = plan.groups * plan.rows, plan.span
    macs = 2 * (2 * rows * u.shape[0] * span + 4 * span * span * rows)
    first, tw, big, last = tables
    sources = (u, first, tw, big, filt, last)
    return pl.pallas_call(
        functools.partial(transform_kernel, plan),
        in_specs=[pl.BlockSpec(memory_space=pl.ANY)] * len(sources),
        out_specs=pl.BlockSpec(memory_space=pltpu.VMEM),
        out_shape=jax.ShapeDtypeStruct(u.shape, BF16),
        scratch_shapes=[pltpu.VMEM(s.shape, s.dtype) for s in sources]
        + [
            pltpu.VMEM((2 * plan.rows, 2 * span), BF16),
            pltpu.VMEM((2 * rows, span), BF16),
            pltpu.SemaphoreType.DMA((len(sources),)),
        ],
        cost_estimate=pl.CostEstimate(flops=2 * macs, bytes_accessed=6 * 1024 * 1024, transcendentals=0),
        compiler_params=pltpu.CompilerParams(vmem_limit_bytes=VMEM_WHOLE),
        name="transform",
    )(*sources)


def final_kernel(y_ref, direct_ref, gate_ref, out_ref):
    conv = y_ref[...].T.astype(F32)
    out_ref[...] = ((conv + direct_ref[...]) * gate_ref[...]).astype(BF16)


def finish(y, direct, gate):
    return pl.pallas_call(
        final_kernel,
        out_shape=jax.ShapeDtypeStruct(direct.shape, BF16),
        cost_estimate=pl.CostEstimate(
            flops=2 * direct.size, bytes_accessed=12 * direct.size, transcendentals=0
        ),
        compiler_params=pltpu.CompilerParams(vmem_limit_bytes=VMEM_LIMIT),
        name="finish",
    )(y, direct, gate)


def exchange(values, axes):
    return lax.all_to_all(values, axes, split_axis=0, concat_axis=0, tiled=True)


def on_device(plan, tables, fold, streams, short_weight, short_bias, spectrum, skip_gain):
    seq = plan.seq
    own = plan.own
    length = streams.shape[1]
    chans = streams.shape[2]
    parts = 4 * spectrum.shape[2]
    sent = transpose_spectrum(spectrum, 8)
    recv = exchange(sent.reshape(-1, own, parts), ("chan", "seq"))
    filt = arrange_filter(plan, recv, fold)

    route = [(i, i + 1) for i in range(seq - 1)]
    halo = lax.ppermute(streams[:, length - 2 :, :], "seq", route)
    ut, direct, gate = short_conv(streams, halo, short_weight, short_bias, skip_gain[None, :])
    mine = exchange(ut.reshape(seq, own, length), "seq").reshape(seq * own, length)
    y = transform(plan, mine, filt, tables)
    back = exchange(y.reshape(seq, own, length), "seq").reshape(chans, length)
    return finish(back, direct, gate)


def solution(mesh):
    seq = mesh.shape["seq"]
    chans = mesh.shape["chan"]
    plan = Plan(seq, chans, 16384, 4096, 1)
    fold = jnp.asarray(plan.fold_table(), BF16)
    tables = (
        jnp.asarray(plan.first_table(), BF16),
        jnp.asarray(plan.twiddle(), F32),
        jnp.asarray(plan.big_table(), BF16),
        jnp.asarray(plan.last_table(), BF16),
    )
    placed = (
        P(None, "seq", "chan"),
        P(None, None, "chan"),
        P(None, "chan"),
        P(None, None, ("chan", "seq"), None),
        P("chan"),
    )
    return jax.shard_map(
        functools.partial(on_device, plan, tables, fold),
        mesh=mesh,
        in_specs=placed,
        out_specs=P("seq", "chan"),
        check_vma=False,
    )
```

time: 102 us -> 96.2 us (0.943)
  Pallas kernels: 20.2 us -> 12.4 us
  waiting for transfers between devices: 33.2 us -> 35.7 us
    pallas_call x5, Pallas kernels: 20.2 us -> 12.4 us  [the longest x1 4.32 us: transform(): pl.pallas_call(functools.partial(transform_kernel, plan), in_specs=[pl.Bl...]
    all_to_all x2, waiting for transfers between devices: 31.9 us -> 34.4 us  [exchange(): return lax.all_to_all(values, axes, split_axis=0, concat_axis=0, tiled=True)]
  transfers between devices with their start and end apart: 3 -> 3, of which waited for: 3 -> 3; matrix products, arithmetic and copies ran while one was open for 1% -> 0% of each run, Pallas kernels for 7% -> 5%
where the time goes in v1:
time: 96.2 us; the launch traced here: 95.8 us
  waiting for transfers between devices  35.7 us (37%)
  starting transfers between devices  30.3 us (31%)
  blocking collectives  15.8 us (16%)
  Pallas kernels  12.4 us (13%)
  local copies, waits for them, and re-layouts  1.54 us (2%)
    all_to_all x2, waiting for transfers between devices, exchange(): return lax.all_to_all(values, axes, split_axis=0, concat_axis=0, tiled=True)  34.4 us
    all_to_all x2, starting transfers between devices, exchange(): return lax.all_to_all(values, axes, split_axis=0, concat_axis=0, tiled=True)  26.9 us
    all_to_all x1, blocking collectives, exchange(): return lax.all_to_all(values, axes, split_axis=0, concat_axis=0, tiled=True)  15.8 us
    pallas_call x1, Pallas kernels, transform(): pl.pallas_call(functools.partial(transform_kernel, plan), in_specs=[pl.Bl...  4.32 us
    ppermute x1, starting transfers between devices, on_device(): halo = lax.ppermute(streams[:, length - 2:, :], 'seq', route)  3.37 us
    pallas_call x1, Pallas kernels, arrange_filter(): pl.pallas_call(functools.partial(filter_kernel, plan), out_shape=jax.Shap...  3.29 us
    pallas_call x1, Pallas kernels, transpose_spectrum(): pl.pallas_call(spectrum_kernel, in_specs=[pl.BlockSpec(memory_space=pl.AN...  2.4 us
  transfers between devices with their start and end apart: 3, of which 3 were waited for; matrix products, arithmetic and copies ran while one was open for 0% of the time, Pallas kernels for 5%

profile of v1, /device:TPU:8, one launch (start us, length us, event | category | flops | bytes accessed | tf_op | source)
XLA Modules:
  0.0 95.8 jit_solution(17712615949080687227)
XLA Ops:
  0.0 2.4 %transpose_spectrum.1 = bf16[4096,128]{1,0:T(8,128)(2,1)} custom-call(bf16[2,2,32,4096]{3,2,1,0:T(8,128)(2,1)} %spec_ref.1), custom_call_target="tpu_custom_call" | custom-call | flops 524288 | bytes 2097152 | tf_op jit(solution)/shard_map/transpose_spectrum/pallas_call | solution.py:117
  2.4 0.0 copy-start
  2.4 0.0 copy-start.1
  2.4 21.1 %all-to-all-start.1 = ((bf16[512,8,128]{2,1,0:T(8,128)(2,1)}), bf16[512,8,128]{2,1,0:T(8,128)(2,1)S(1)}, u32[]{:S(2)}, u32[]{:S(2)}) async-start(bf16[512,8,128]{2,1,0:T(8,128)(2,1)} %bitcast.8), calls=%async_computation.1 | async-start | bytes 2097152 | tf_op jit(solution)/shard_map/all_to_all | solution.py:303
  23.6 0.0 copy-done
  23.6 0.0 copy-start.2
  23.6 0.0 copy-start.3
  23.6 3.4 %collective-permute-start = (bf16[3,2,256]{2,1,0:T(2,128)(2,1)S(1)}, bf16[3,2,256]{2,1,0:T(2,128)(2,1)S(1)}, u32[]{:S(2)}, u32[]{:S(2)}) collective-permute-start(bf16[3,2,256]{2,1,0:T(2,128)(2,1)S(1)} %slice.3), channel_id=1, source_target_pairs={{0,16},{16,32},{32,48},{48,64},{64,80},{80,96},{96,112},{112,128},... | collective-permute-start | bytes 9224 | tf_op jit(solution)/shard_map/ppermute | solution.py:317
  27.0 1.3 %collective-permute-done.halo_ref = bf16[3,2,256]{2,1,0:T(2,128)(2,1)S(1)} collective-permute-done((bf16[3,2,256]{2,1,0:T(2,128)(2,1)S(1)}, bf16[3,2,256]{2,1,0:T(2,128)(2,1)S(1)}, u32[]{:S(2)}, u32[]{:S(2)}) %collective-permute-start) | collective-permute-done | bytes 3104 | tf_op jit(solution)/shard_map/ppermute | solution.py:317
  28.3 0.0 copy-done.1
  28.3 0.0 copy-done.2
  28.3 0.0 copy-done.3
  28.3 1.5 %short_conv.1 = (bf16[256,512]{1,0:T(8,128)(2,1)}, f32[512,256]{1,0:T(8,128)S(1)}, f32[512,256]{1,0:T(8,128)S(1)}) custom-call(bf16[3,512,256]{2,1,0:T(8,128)(2,1)S(1)} %copy-done, bf16[3,2,256]{2,1,0:T(2,128)(2,1)S(1)} %collective-permute-done.halo_ref, f32[3,3,256]{2,1,0:T(4,128)S(1)} %copy-done.1, f32[3,256]{1,0:T(4,128)S(1)} %copy-done.2, ...), custom_call_target="tpu_custom_call" | custom-call | flops 2621440 | bytes 2097152 | tf_op jit(solution)/shard_map/short_conv/pallas_call | solution.py:158
  29.8 26.1 %all-to-all-done.1.recv_ref = bf16[512,8,128]{2,1,0:T(8,128)(2,1)S(1)} async-done(((bf16[512,8,128]{2,1,0:T(8,128)(2,1)}), bf16[512,8,128]{2,1,0:T(8,128)(2,1)S(1)}, u32[]{:S(2)}, u32[]{:S(2)}) %all-to-all-start.1) | async-done | bytes 1048608 | tf_op jit(solution)/shard_map/all_to_all | solution.py:303
  56.0 0.0 copy-start.4
  56.0 5.8 %all-to-all-start = ((bf16[32,8,512]{2,1,0:T(8,128)(2,1)}), bf16[32,8,512]{2,1,0:T(8,128)(2,1)S(1)}, u32[]{:S(2)}, u32[]{:S(2)}) async-start(bf16[32,8,512]{2,1,0:T(8,128)(2,1)} %bitcast.1), calls=%async_computation | async-start | bytes 524288 | tf_op jit(solution)/shard_map/all_to_all | solution.py:303
  61.8 0.0 copy-done.4
  61.8 3.3 %arrange_filter.1.refs_4_ = bf16[544,512]{1,0:T(8,128)(2,1)S(1)} custom-call(bf16[512,8,128]{2,1,0:T(8,128)(2,1)S(1)} %all-to-all-done.1.recv_ref, bf16[72,256]{1,0:T(8,128)(2,1)S(1)} %copy-done.4), custom_call_target="tpu_custom_call" | custom-call | flops 536870912 | bytes 3145728 | tf_op jit(solution)/shard_map/arrange_filter/pallas_call | solution.py:198
  65.1 0.0 copy-start.5
  65.1 0.8 copy-done.5
  65.9 8.2 %all-to-all-done = bf16[32,8,512]{2,1,0:T(8,128)(2,1)S(1)} async-done(((bf16[32,8,512]{2,1,0:T(8,128)(2,1)}), bf16[32,8,512]{2,1,0:T(8,128)(2,1)S(1)}, u32[]{:S(2)}, u32[]{:S(2)}) %all-to-all-start) | async-done | bytes 262176 | tf_op jit(solution)/shard_map/all_to_all | solution.py:303
  74.2 0.0 copy-start.6
  74.2 0.7 copy-done.6
  74.9 4.3 %transform.1 = bf16[256,512]{1,0:T(8,128)(2,1)} custom-call(bf16[256,512]{1,0:T(8,128)(2,1)} %bitcast.9, bf16[544,256]{1,0:T(8,128)(2,1)} %constant.11.clone.refs_1_, f32[2,48,512]{2,1,0:T(8,128)} %constant.12.clone.refs_2_, bf16[1024,512]{1,0:T(8,128)(2,1)} %constant.13.clone.refs_3_, bf16[544,512]{1,0:T(8,128)(2,1)} %copy-done.5, ...), custom_call_target="tpu_custom_call" | custom-call | flops 1426063360 | bytes 6291456 | tf_op jit(solution)/shard_map/transform/pallas_call | solution.py:268
  79.2 15.8 %all_to_all.15 = bf16[32,8,512]{2,1,0:T(8,128)(2,1)S(1)} all-to-all(bf16[32,8,512]{2,1,0:T(8,128)(2,1)} %bitcast.10), channel_id=1, replica_groups=mesh['seq'=32,'chan'=16] {'seq'}, dimensions={0} | all-to-all | bytes 524288 | tf_op jit(solution)/shard_map/all_to_all | solution.py:303
  95.0 0.8 finish.1
  (1 shorter events, 0.0 us)
Async XLA Ops:
  2.4 21.1 %copy-start = (bf16[3,512,256]{2,1,0:T(8,128)(2,1)S(1)}, bf16[3,512,256]{2,1,0:T(8,128)(2,1)}, u32[]{:S(2)}) copy-start(bf16[3,512,256]{2,1,0:T(8,128)(2,1)} %streams_ref.1) | copy-start | bytes 2359300
  2.4 25.9 %copy-start.1 = (f32[3,3,256]{2,1,0:T(4,128)S(1)}, f32[3,3,256]{2,1,0:T(4,128)}, u32[]{:S(2)}) copy-start(f32[3,3,256]{2,1,0:T(4,128)} %weight_ref.1) | copy-start | bytes 27652
  2.4 53.6 %all-to-all-start.1 = ((bf16[512,8,128]{2,1,0:T(8,128)(2,1)}), bf16[512,8,128]{2,1,0:T(8,128)(2,1)S(1)}, u32[]{:S(2)}, u32[]{:S(2)}) async-start(bf16[512,8,128]{2,1,0:T(8,128)(2,1)} %bitcast.8), calls=%async_computation.1 | async-start | bytes 2097152 | tf_op jit(solution)/shard_map/all_to_all | solution.py:303
  23.6 4.7 %copy-start.2 = (f32[3,256]{1,0:T(4,128)S(1)}, f32[3,256]{1,0:T(4,128)}, u32[]{:S(2)}) copy-start(f32[3,256]{1,0:T(4,128)} %bias_ref.1) | copy-start | bytes 9220
  23.6 4.7 %copy-start.3 = (f32[256]{0:T(256)S(1)}, f32[256]{0:T(256)}, u32[]{:S(2)}) copy-start(f32[256]{0:T(256)} %param.14) | copy-start | bytes 3076
  23.6 4.7 %collective-permute-start = (bf16[3,2,256]{2,1,0:T(2,128)(2,1)S(1)}, bf16[3,2,256]{2,1,0:T(2,128)(2,1)S(1)}, u32[]{:S(2)}, u32[]{:S(2)}) collective-permute-start(bf16[3,2,256]{2,1,0:T(2,128)(2,1)S(1)} %slice.3), channel_id=1, source_target_pairs={{0,16},{16,32},{32,48},{48,64},{64,80},{80,96},{96,112},{112,128},... | collective-permute-start | bytes 9224 | tf_op jit(solution)/shard_map/ppermute | solution.py:317
  56.0 5.8 %copy-start.4 = (bf16[72,256]{1,0:T(8,128)(2,1)S(1)}, bf16[72,256]{1,0:T(8,128)(2,1)}, u32[]{:S(2)}) copy-start(bf16[72,256]{1,0:T(8,128)(2,1)} %constant.10.clone.fold_ref) | copy-start | bytes 110596
  56.0 18.2 %all-to-all-start = ((bf16[32,8,512]{2,1,0:T(8,128)(2,1)}), bf16[32,8,512]{2,1,0:T(8,128)(2,1)S(1)}, u32[]{:S(2)}, u32[]{:S(2)}) async-start(bf16[32,8,512]{2,1,0:T(8,128)(2,1)} %bitcast.1), calls=%async_computation | async-start | bytes 524288 | tf_op jit(solution)/shard_map/all_to_all | solution.py:303
  65.1 0.8 copy-start.5
  74.2 0.7 copy-start.6

commit v2 on v1

--- a/solution.py
+++ b/solution.py
@@ -11,7 +11,7 @@
 F32 = jnp.float32
 BF16 = jnp.bfloat16
 VMEM_LIMIT = 20 * 1024 * 1024
-VMEM_WHOLE = 56 * 1024 * 1024
+VMEM_WHOLE = 53 * 1024 * 1024
 
 
 def dot_t(lhs, rhs):
@@ -211,7 +211,12 @@
     count = 6
     sources, y_ref, held = refs[:count], refs[count], refs[count + 1 : 2 * count + 1]
     left_ref, b_ref, sems = refs[2 * count + 1 :]
-    fetches = [pltpu.make_async_copy(s, h, sems.at[j]) for j, (s, h) in enumerate(zip(sources, held))]
+    fetches = [
+        pltpu.make_async_copy(
+            s.at[:, : h.shape[1]] if len(h.shape) == 3 else s, h, sems.at[j]
+        )
+        for j, (s, h) in enumerate(zip(sources, held))
+    ]
     for fetch in fetches:
         fetch.start()
     u_ref, first_ref, tw_ref, big_ref, filt_ref, last_ref = held
@@ -270,7 +275,9 @@
         in_specs=[pl.BlockSpec(memory_space=pl.ANY)] * len(sources),
         out_specs=pl.BlockSpec(memory_space=pltpu.VMEM),
         out_shape=jax.ShapeDtypeStruct(u.shape, BF16),
-        scratch_shapes=[pltpu.VMEM(s.shape, s.dtype) for s in sources]
+        scratch_shapes=[pltpu.VMEM(s.shape, s.dtype) for s in (u, first)]
+        + [pltpu.VMEM((2, plan.seq + plan.spare, span), F32)]
+        + [pltpu.VMEM(s.shape, s.dtype) for s in (big, filt, last)]
         + [
             pltpu.VMEM((2 * plan.rows, 2 * span), BF16),
             pltpu.VMEM((2 * rows, span), BF16),
@@ -309,7 +316,7 @@
     length = streams.shape[1]
     chans = streams.shape[2]
     parts = 4 * spectrum.shape[2]
-    sent = transpose_spectrum(spectrum, 8)
+    sent = transpose_spectrum(spectrum, 4)
     recv = exchange(sent.reshape(-1, own, parts), ("chan", "seq"))
     filt = arrange_filter(plan, recv, fold)
 
@@ -329,7 +336,7 @@
     fold = jnp.asarray(plan.fold_table(), BF16)
     tables = (
         jnp.asarray(plan.first_table(), BF16),
-        jnp.asarray(plan.twiddle(), F32),
+        jnp.asarray(np.pad(plan.twiddle(), ((0, 0), (0, 48), (0, 0))), F32),
         jnp.asarray(plan.big_table(), BF16),
         jnp.asarray(plan.last_table(), BF16),
     )

time: 96.2 us -> 94.3 us (0.980)
  Pallas kernels: 12.4 us -> 11.4 us
where the time goes in v2:
time: 94.3 us; the launch traced here: 93.9 us
  waiting for transfers between devices  35.7 us (38%)
  starting transfers between devices  30.3 us (32%)
  blocking collectives  15.6 us (17%)
  Pallas kernels  11.4 us (12%)
    all_to_all x2, waiting for transfers between devices, exchange(): return lax.all_to_all(values, axes, split_axis=0, concat_axis=0, tiled=True)  34.4 us
    all_to_all x2, starting transfers between devices, exchange(): return lax.all_to_all(values, axes, split_axis=0, concat_axis=0, tiled=True)  26.9 us
    all_to_all x1, blocking collectives, exchange(): return lax.all_to_all(values, axes, split_axis=0, concat_axis=0, tiled=True)  15.6 us
    pallas_call x1, Pallas kernels, transform(): pl.pallas_call(functools.partial(transform_kernel, plan), in_specs=[pl.Bl...  3.54 us
    ppermute x1, starting transfers between devices, on_device(): halo = lax.ppermute(streams[:, length - 2:, :], 'seq', route)  3.37 us
    pallas_call x1, Pallas kernels, arrange_filter(): pl.pallas_call(functools.partial(filter_kernel, plan), out_shape=jax.Shap...  3.29 us
    pallas_call x1, Pallas kernels, transpose_spectrum(): pl.pallas_call(spectrum_kernel, in_specs=[pl.BlockSpec(memory_space=pl.AN...  2.23 us
  transfers between devices with their start and end apart: 3, of which 3 were waited for; matrix products, arithmetic and copies ran while one was open for 0% of the time, Pallas kernels for 5%

profile of v2, /device:TPU:8, one launch (start us, length us, event | category | flops | bytes accessed | tf_op | source)
XLA Modules:
  0.0 93.9 jit_solution(6596631879827360996)
XLA Ops:
  0.0 2.2 %transpose_spectrum.1 = bf16[4096,128]{1,0:T(8,128)(2,1)} custom-call(bf16[2,2,32,4096]{3,2,1,0:T(8,128)(2,1)} %spec_ref.1), custom_call_target="tpu_custom_call" | custom-call | flops 524288 | bytes 2097152 | tf_op jit(solution)/shard_map/transpose_spectrum/pallas_call | solution.py:117
  2.2 0.0 copy-start
  2.3 0.0 copy-start.1
  2.3 21.1 %all-to-all-start.1 = ((bf16[512,8,128]{2,1,0:T(8,128)(2,1)}), bf16[512,8,128]{2,1,0:T(8,128)(2,1)S(1)}, u32[]{:S(2)}, u32[]{:S(2)}) async-start(bf16[512,8,128]{2,1,0:T(8,128)(2,1)} %bitcast.10), calls=%async_computation.1 | async-start | bytes 2097152 | tf_op jit(solution)/shard_map/all_to_all | solution.py:310
  23.4 0.0 copy-done
  23.4 0.0 copy-start.2
  23.4 0.0 copy-start.3
  23.4 3.4 %collective-permute-start = (bf16[3,2,256]{2,1,0:T(2,128)(2,1)S(1)}, bf16[3,2,256]{2,1,0:T(2,128)(2,1)S(1)}, u32[]{:S(2)}, u32[]{:S(2)}) collective-permute-start(bf16[3,2,256]{2,1,0:T(2,128)(2,1)S(1)} %slice.3), channel_id=1, source_target_pairs={{0,16},{16,32},{32,48},{48,64},{64,80},{80,96},{96,112},{112,128},... | collective-permute-start | bytes 9224 | tf_op jit(solution)/shard_map/ppermute | solution.py:324
  26.8 1.3 %collective-permute-done.halo_ref = bf16[3,2,256]{2,1,0:T(2,128)(2,1)S(1)} collective-permute-done((bf16[3,2,256]{2,1,0:T(2,128)(2,1)S(1)}, bf16[3,2,256]{2,1,0:T(2,128)(2,1)S(1)}, u32[]{:S(2)}, u32[]{:S(2)}) %collective-permute-start) | collective-permute-done | bytes 3104 | tf_op jit(solution)/shard_map/ppermute | solution.py:324
  28.1 0.0 copy-done.1
  28.1 0.0 copy-done.2
  28.1 0.0 copy-done.3
  28.1 1.5 %short_conv.1 = (bf16[256,512]{1,0:T(8,128)(2,1)}, f32[512,256]{1,0:T(8,128)S(1)}, f32[512,256]{1,0:T(8,128)S(1)}) custom-call(bf16[3,512,256]{2,1,0:T(8,128)(2,1)S(1)} %copy-done, bf16[3,2,256]{2,1,0:T(2,128)(2,1)S(1)} %collective-permute-done.halo_ref, f32[3,3,256]{2,1,0:T(4,128)S(1)} %copy-done.1, f32[3,256]{1,0:T(4,128)S(1)} %copy-done.2, ...), custom_call_target="tpu_custom_call" | custom-call | flops 2621440 | bytes 2097152 | tf_op jit(solution)/shard_map/short_conv/pallas_call | solution.py:158
  29.7 26.1 %all-to-all-done.1.recv_ref = bf16[512,8,128]{2,1,0:T(8,128)(2,1)S(1)} async-done(((bf16[512,8,128]{2,1,0:T(8,128)(2,1)}), bf16[512,8,128]{2,1,0:T(8,128)(2,1)S(1)}, u32[]{:S(2)}, u32[]{:S(2)}) %all-to-all-start.1) | async-done | bytes 1048608 | tf_op jit(solution)/shard_map/all_to_all | solution.py:310
  55.8 0.0 copy-start.5
  55.8 5.8 %all-to-all-start = ((bf16[32,8,512]{2,1,0:T(8,128)(2,1)}), bf16[32,8,512]{2,1,0:T(8,128)(2,1)S(1)}, u32[]{:S(2)}, u32[]{:S(2)}) async-start(bf16[32,8,512]{2,1,0:T(8,128)(2,1)} %bitcast.1), calls=%async_computation | async-start | bytes 524288 | tf_op jit(solution)/shard_map/all_to_all | solution.py:310
  61.6 0.0 copy-done.5
  61.6 0.0 copy-start.4
  61.7 3.3 %arrange_filter.1.refs_4_ = bf16[544,512]{1,0:T(8,128)(2,1)S(1)} custom-call(bf16[512,8,128]{2,1,0:T(8,128)(2,1)S(1)} %all-to-all-done.1.recv_ref, bf16[72,256]{1,0:T(8,128)(2,1)S(1)} %copy-done.5), custom_call_target="tpu_custom_call" | custom-call | flops 536870912 | bytes 3145728 | tf_op jit(solution)/shard_map/arrange_filter/pallas_call | solution.py:198
  65.0 0.0 copy-start.6
  65.0 0.8 copy-done.6
  65.8 8.2 %all-to-all-done = bf16[32,8,512]{2,1,0:T(8,128)(2,1)S(1)} async-done(((bf16[32,8,512]{2,1,0:T(8,128)(2,1)}), bf16[32,8,512]{2,1,0:T(8,128)(2,1)S(1)}, u32[]{:S(2)}, u32[]{:S(2)}) %all-to-all-start) | async-done | bytes 262176 | tf_op jit(solution)/shard_map/all_to_all | solution.py:310
  74.0 0.0 copy-done.4
  74.0 3.5 %transform.1 = bf16[256,512]{1,0:T(8,128)(2,1)S(1)} custom-call(bf16[256,512]{1,0:T(8,128)(2,1)S(1)} %bitcast.7, bf16[544,256]{1,0:T(8,128)(2,1)S(1)} %copy-done.4, f32[2,96,512]{2,1,0:T(8,128)} %constant.12.clone.refs_2_, bf16[1024,512]{1,0:T(8,128)(2,1)} %constant.13.clone.refs_3_, bf16[544,512]{1,0:T(8,128)(2,1)} %copy-done.6, ...), custom_call_target="tpu_custom_call" | custom-call | flops 1426063360 | bytes 6291456 | tf_op jit(solution)/shard_map/transform/pallas_call | solution.py:273
  77.5 15.6 %all_to_all.15 = bf16[32,8,512]{2,1,0:T(8,128)(2,1)S(1)} all-to-all(bf16[32,8,512]{2,1,0:T(8,128)(2,1)S(1)} %bitcast.8), channel_id=1, replica_groups=mesh['seq'=32,'chan'=16] {'seq'}, dimensions={0} | all-to-all | bytes 524288 | tf_op jit(solution)/shard_map/all_to_all | solution.py:310
  93.1 0.8 finish.1
  (1 shorter events, 0.0 us)
Async XLA Ops:
  2.2 21.1 %copy-start = (bf16[3,512,256]{2,1,0:T(8,128)(2,1)S(1)}, bf16[3,512,256]{2,1,0:T(8,128)(2,1)}, u32[]{:S(2)}) copy-start(bf16[3,512,256]{2,1,0:T(8,128)(2,1)} %streams_ref.1) | copy-start | bytes 2359300
  2.3 25.9 %copy-start.1 = (f32[3,3,256]{2,1,0:T(4,128)S(1)}, f32[3,3,256]{2,1,0:T(4,128)}, u32[]{:S(2)}) copy-start(f32[3,3,256]{2,1,0:T(4,128)} %weight_ref.1) | copy-start | bytes 27652
  2.3 53.6 %all-to-all-start.1 = ((bf16[512,8,128]{2,1,0:T(8,128)(2,1)}), bf16[512,8,128]{2,1,0:T(8,128)(2,1)S(1)}, u32[]{:S(2)}, u32[]{:S(2)}) async-start(bf16[512,8,128]{2,1,0:T(8,128)(2,1)} %bitcast.10), calls=%async_computation.1 | async-start | bytes 2097152 | tf_op jit(solution)/shard_map/all_to_all | solution.py:310
  23.4 4.7 %copy-start.2 = (f32[3,256]{1,0:T(4,128)S(1)}, f32[3,256]{1,0:T(4,128)}, u32[]{:S(2)}) copy-start(f32[3,256]{1,0:T(4,128)} %bias_ref.1) | copy-start | bytes 9220
  23.4 4.7 %copy-start.3 = (f32[256]{0:T(256)S(1)}, f32[256]{0:T(256)}, u32[]{:S(2)}) copy-start(f32[256]{0:T(256)} %param.14) | copy-start | bytes 3076
  23.4 4.7 %collective-permute-start = (bf16[3,2,256]{2,1,0:T(2,128)(2,1)S(1)}, bf16[3,2,256]{2,1,0:T(2,128)(2,1)S(1)}, u32[]{:S(2)}, u32[]{:S(2)}) collective-permute-start(bf16[3,2,256]{2,1,0:T(2,128)(2,1)S(1)} %slice.3), channel_id=1, source_target_pairs={{0,16},{16,32},{32,48},{48,64},{64,80},{80,96},{96,112},{112,128},... | collective-permute-start | bytes 9224 | tf_op jit(solution)/shard_map/ppermute | solution.py:324
  55.8 5.8 %copy-start.5 = (bf16[72,256]{1,0:T(8,128)(2,1)S(1)}, bf16[72,256]{1,0:T(8,128)(2,1)}, u32[]{:S(2)}) copy-start(bf16[72,256]{1,0:T(8,128)(2,1)} %constant.10.clone.fold_ref) | copy-start | bytes 110596
  55.8 18.2 %all-to-all-start = ((bf16[32,8,512]{2,1,0:T(8,128)(2,1)}), bf16[32,8,512]{2,1,0:T(8,128)(2,1)S(1)}, u32[]{:S(2)}, u32[]{:S(2)}) async-start(bf16[32,8,512]{2,1,0:T(8,128)(2,1)} %bitcast.1), calls=%async_computation | async-start | bytes 524288 | tf_op jit(solution)/shard_map/all_to_all | solution.py:310
  61.6 12.3 %copy-start.4 = (bf16[544,256]{1,0:T(8,128)(2,1)S(1)}, bf16[544,256]{1,0:T(8,128)(2,1)}, u32[]{:S(2)}) copy-start(bf16[544,256]{1,0:T(8,128)(2,1)} %constant.11.clone.refs_1_) | copy-start | bytes 835588
  65.0 0.8 copy-start.6

commit v3 on v2

--- a/solution.py
+++ b/solution.py
@@ -58,32 +58,35 @@
         return table.reshape(-1, self.seq * self.own).T
 
     def big_table(self):
-        d = np.arange(self.span)
-        angle = 2.0 * np.pi * ((d[:, None] * d[None, :]) % self.span) / self.span
+        half = self.span // 2
+        d = np.arange(half)
+        angle = 2.0 * np.pi * ((d[:, None] * d[None, :]) % half) / half
         return np.concatenate([np.cos(angle), np.sin(angle)])
 
     def twiddle(self):
         low = np.append(self.lows, [self.seq] * self.spare)
         a = np.arange(self.span)
         angle = 2.0 * np.pi * ((low[:, None] * a[None, :]) % self.total) / self.total
+        step = np.tile(2.0 * np.pi * a / self.span, (8, 1))
+        angle = np.concatenate([angle, step])
         return np.stack([np.cos(angle), np.sin(angle)])
 
     def fold_table(self):
         half = self.seq
         lanes = 4 * self.seq
-        out = np.zeros((2 * self.seq + 8, 2 * lanes))
+        out = np.zeros((2, 2 * self.seq + self.spare, lanes))
 
         def lane(part, low):
             return part * 2 * half + (low % 2) * half + low // 2
 
         for q, low in enumerate(self.lows):
             for part in range(2):
-                out[part * self.seq + q, lane(part, low)] = 1.0
+                out[0, part * self.seq + q, lane(part, low)] = 1.0
                 if low:
-                    out[part * self.seq + q, lanes + lane(part, 2 * self.seq - low)] = 1.0 - 2.0 * part
+                    out[1, part * self.seq + q, lane(part, 2 * self.seq - low)] = 1.0 - 2.0 * part
         for part in range(2):
-            out[2 * self.seq + part, lane(part, self.seq)] = 1.0
-        return out
+            out[0, 2 * self.seq + part, lane(part, self.seq)] = 1.0
+        return out.reshape(-1, lanes)
 
 
 def spectrum_kernel(spec_ref, out_ref, held_ref, turned_ref, in_sems, out_sems):
@@ -170,22 +173,29 @@
     )(streams, halo, weight, bias, skip)
 
 
-def filter_kernel(plan, recv_ref, fold_ref, out_ref, wide_ref):
+def filter_kernel(plan, recv_ref, fold_ref, out_ref, wide_ref, both_ref):
     depth = recv_ref.shape[0]
     seq, rows, base = plan.seq, plan.rows, plan.base
     wide_ref[...] = recv_ref[...].astype(F32)
     row = lax.broadcasted_iota(jnp.int32, (depth, depth), 0)
     column = lax.broadcasted_iota(jnp.int32, (depth, depth), 1)
-    reverse = jnp.where(row + column == depth - 1, 1.0, 0.0).astype(BF16)
+    source = jnp.where(column < depth // 2, 2 * column, 2 * column - depth + 1)
+    forth = jnp.where(row == source, 1.0, 0.0)
+    reverse = jnp.where(row + source == depth - 1, 1.0, 0.0)
+    order = jnp.concatenate([forth, reverse], axis=0).astype(BF16)
     for g in range(plan.groups):
         for part in range(2):
             first = (2 * g + part) * rows + base
             out_ref[first : first + plan.spare, :] = jnp.zeros((plan.spare, depth), BF16)
+    each = fold_ref.shape[0] // 2
+    for ch in range(plan.own):
+        picked = dot(fold_ref[...], wide_ref[:, ch, :].astype(BF16).T).astype(BF16)
+        both_ref[ch * each : (ch + 1) * each, :depth] = picked[:each]
+        both_ref[ch * each : (ch + 1) * each, depth:] = picked[each:]
+    sums = dot(both_ref[...], order).astype(BF16)
     for ch in range(plan.own):
         g, c = divmod(ch, plan.members)
-        turned = wide_ref[:, ch, :].astype(BF16).T
-        back = dot(turned, reverse).astype(BF16)
-        folded = dot(fold_ref[...], jnp.concatenate([turned, back], axis=0)).astype(BF16)
+        folded = sums[ch * each : (ch + 1) * each]
         for part in range(2):
             first = (2 * g + part) * rows
             out_ref[first + c * seq : first + (c + 1) * seq, :] = folded[part * seq : (part + 1) * seq]
@@ -198,7 +208,10 @@
     return pl.pallas_call(
         functools.partial(filter_kernel, plan),
         out_shape=jax.ShapeDtypeStruct((2 * plan.groups * plan.rows, depth), BF16),
-        scratch_shapes=[pltpu.VMEM((depth, own, lanes), F32)],
+        scratch_shapes=[
+            pltpu.VMEM((depth, own, lanes), F32),
+            pltpu.VMEM((own * fold.shape[0] // 2, 2 * depth), BF16),
+        ],
         cost_estimate=pl.CostEstimate(
             flops=2 * depth * own * lanes * depth, bytes_accessed=6 * depth * own * lanes, transcendentals=0
         ),
@@ -229,6 +242,8 @@
     ]
     fetches[2].wait()
 
+    half = span // 2
+
     def turn(re, im):
         parts = []
         for at in list(range(0, base, seq)) + [base]:
@@ -238,36 +253,54 @@
             s = tw_ref[1, first : first + size, :]
             r, i = re[at : at + size], im[at : at + size]
             parts.append((r * c - i * s, r * s + i * c))
-        return [jnp.concatenate(p, axis=0).astype(BF16) for p in zip(*parts)]
-
-    def multiply(re, im):
-        left_ref[:rows, :span] = re
-        left_ref[:rows, span:] = -im
-        left_ref[rows:, :span] = im
-        left_ref[rows:, span:] = re
+        return [jnp.concatenate(p, axis=0) for p in zip(*parts)]
+
+    def step(re, im):
+        c = tw_ref[0, seq + plan.spare : seq + plan.spare + 1, :half]
+        s = tw_ref[1, seq + plan.spare : seq + plan.spare + 1, :half]
+        return re * c - im * s, re * s + im * c
+
+    def multiply(pairs):
+        for j, (re, im) in enumerate(pairs):
+            at = 2 * j * rows
+            re, im = re.astype(BF16), im.astype(BF16)
+            left_ref[at : at + rows, :half] = re
+            left_ref[at : at + rows, half:] = -im
+            left_ref[at + rows : at + 2 * rows, :half] = im
+            left_ref[at + rows : at + 2 * rows, half:] = re
         out = dot(left_ref[...], big_ref[...])
-        return out[:rows], out[rows:]
+        return [
+            (out[2 * j * rows : (2 * j + 1) * rows], out[(2 * j + 1) * rows : (2 * j + 2) * rows])
+            for j in range(len(pairs))
+        ]
 
     turned = [turn(stage[:rows], stage[rows:]) for stage in stages]
     fetches[3].wait()
     fetches[4].wait()
     for g in range(plan.groups):
         lo, mid, hi = (2 * g) * rows, (2 * g + 1) * rows, (2 * g + 2) * rows
-        xr, xi = multiply(*turned[g])
-        hr = filt_ref[lo:mid, :].astype(F32)
-        h_im = filt_ref[mid:hi, :].astype(F32)
-        yr = (hr * xr + h_im * xi).astype(BF16)
-        yi = (h_im * xr - hr * xi).astype(BF16)
-        br, bi = turn(*multiply(yr, yi))
-        b_ref[lo:mid, :] = br
-        b_ref[mid:hi, :] = bi
+        re, im = turned[g]
+        even = (re[:, :half] + re[:, half:], im[:, :half] + im[:, half:])
+        odd = step(re[:, :half] - re[:, half:], im[:, :half] - im[:, half:])
+        weighted = []
+        for j, (xr, xi) in enumerate(multiply([even, odd])):
+            hr = filt_ref[lo:mid, j * half : (j + 1) * half].astype(F32)
+            hi_part = filt_ref[mid:hi, j * half : (j + 1) * half].astype(F32)
+            weighted.append((hr * xr + hi_part * xi, hi_part * xr - hr * xi))
+        (er, ei), odd = multiply(weighted)
+        sr, si = step(*odd)
+        br, bi = turn(
+            jnp.concatenate([er + sr, er - sr], axis=1), jnp.concatenate([ei + si, ei - si], axis=1)
+        )
+        b_ref[lo:mid, :] = br.astype(BF16)
+        b_ref[mid:hi, :] = bi.astype(BF16)
     fetches[5].wait()
     y_ref[...] = dot(last_ref[...], b_ref[...]).astype(BF16)
 
 
 def transform(plan, u, filt, tables):
     rows, span = plan.groups * plan.rows, plan.span
-    macs = 2 * (2 * rows * u.shape[0] * span + 4 * span * span * rows)
+    macs = 2 * (2 * rows * u.shape[0] * span + 2 * span * span * rows)
     first, tw, big, last = tables
     sources = (u, first, tw, big, filt, last)
     return pl.pallas_call(
@@ -276,10 +309,10 @@
         out_specs=pl.BlockSpec(memory_space=pltpu.VMEM),
         out_shape=jax.ShapeDtypeStruct(u.shape, BF16),
         scratch_shapes=[pltpu.VMEM(s.shape, s.dtype) for s in (u, first)]
-        + [pltpu.VMEM((2, plan.seq + plan.spare, span), F32)]
+        + [pltpu.VMEM((2, plan.seq + plan.spare + 8, span), F32)]
         + [pltpu.VMEM(s.shape, s.dtype) for s in (big, filt, last)]
         + [
-            pltpu.VMEM((2 * plan.rows, 2 * span), BF16),
+            pltpu.VMEM((4 * plan.rows, span), BF16),
             pltpu.VMEM((2 * rows, span), BF16),
             pltpu.SemaphoreType.DMA((len(sources),)),
         ],
@@ -336,7 +369,7 @@
     fold = jnp.asarray(plan.fold_table(), BF16)
     tables = (
         jnp.asarray(plan.first_table(), BF16),
-        jnp.asarray(np.pad(plan.twiddle(), ((0, 0), (0, 48), (0, 0))), F32),
+        jnp.asarray(np.pad(plan.twiddle(), ((0, 0), (0, 40), (0, 0))), F32),
         jnp.asarray(plan.big_table(), BF16),
         jnp.asarray(plan.last_table(), BF16),
     )

time: 94.3 us -> 94 us (level)
  no operation moved by 1% of the time
where the time goes in v3:
time: 94 us; the launch traced here: 93.6 us
  waiting for transfers between devices  35.8 us (38%)
  starting transfers between devices  30.3 us (32%)
  blocking collectives  15.6 us (17%)
  Pallas kernels  11 us (12%)
    all_to_all x2, waiting for transfers between devices, exchange(): return lax.all_to_all(values, axes, split_axis=0, concat_axis=0, tiled=True)  34.5 us
    all_to_all x2, starting transfers between devices, exchange(): return lax.all_to_all(values, axes, split_axis=0, concat_axis=0, tiled=True)  26.9 us
    all_to_all x1, blocking collectives, exchange(): return lax.all_to_all(values, axes, split_axis=0, concat_axis=0, tiled=True)  15.6 us
    ppermute x1, starting transfers between devices, on_device(): halo = lax.ppermute(streams[:, length - 2:, :], 'seq', route)  3.37 us
    pallas_call x1, Pallas kernels, transform(): pl.pallas_call(functools.partial(transform_kernel, plan), in_specs=[pl.Bl...  3.24 us
    pallas_call x1, Pallas kernels, arrange_filter(): pl.pallas_call(functools.partial(filter_kernel, plan), out_shape=jax.Shap...  3.16 us
    pallas_call x1, Pallas kernels, transpose_spectrum(): pl.pallas_call(spectrum_kernel, in_specs=[pl.BlockSpec(memory_space=pl.AN...  2.23 us
  transfers between devices with their start and end apart: 3, of which 3 were waited for; matrix products, arithmetic and copies ran while one was open for 0% of the time, Pallas kernels for 5%

profile of v3, /device:TPU:8, one launch (start us, length us, event | category | flops | bytes accessed | tf_op | source)
XLA Modules:
  0.0 93.6 jit_solution(1806252159299840457)
XLA Ops:
  0.0 2.2 %transpose_spectrum.1 = bf16[4096,128]{1,0:T(8,128)(2,1)} custom-call(bf16[2,2,32,4096]{3,2,1,0:T(8,128)(2,1)} %spec_ref.1), custom_call_target="tpu_custom_call" | custom-call | flops 524288 | bytes 2097152 | tf_op jit(solution)/shard_map/transpose_spectrum/pallas_call | solution.py:120
  2.2 0.0 copy-start
  2.3 0.0 copy-start.1
  2.3 21.1 %all-to-all-start.1 = ((bf16[512,8,128]{2,1,0:T(8,128)(2,1)}), bf16[512,8,128]{2,1,0:T(8,128)(2,1)S(1)}, u32[]{:S(2)}, u32[]{:S(2)}) async-start(bf16[512,8,128]{2,1,0:T(8,128)(2,1)} %bitcast.10), calls=%async_computation.1 | async-start | bytes 2097152 | tf_op jit(solution)/shard_map/all_to_all | solution.py:343
  23.4 0.0 copy-done
  23.4 0.0 copy-start.2
  23.4 0.0 copy-start.3
  23.4 3.4 %collective-permute-start = (bf16[3,2,256]{2,1,0:T(2,128)(2,1)S(1)}, bf16[3,2,256]{2,1,0:T(2,128)(2,1)S(1)}, u32[]{:S(2)}, u32[]{:S(2)}) collective-permute-start(bf16[3,2,256]{2,1,0:T(2,128)(2,1)S(1)} %slice.3), channel_id=1, source_target_pairs={{0,16},{16,32},{32,48},{48,64},{64,80},{80,96},{96,112},{112,128},... | collective-permute-start | bytes 9224 | tf_op jit(solution)/shard_map/ppermute | solution.py:357
  26.8 1.3 %collective-permute-done.halo_ref = bf16[3,2,256]{2,1,0:T(2,128)(2,1)S(1)} collective-permute-done((bf16[3,2,256]{2,1,0:T(2,128)(2,1)S(1)}, bf16[3,2,256]{2,1,0:T(2,128)(2,1)S(1)}, u32[]{:S(2)}, u32[]{:S(2)}) %collective-permute-start) | collective-permute-done | bytes 3104 | tf_op jit(solution)/shard_map/ppermute | solution.py:357
  28.1 0.0 copy-done.1
  28.1 0.0 copy-done.2
  28.1 0.0 copy-done.3
  28.1 1.5 %short_conv.1 = (bf16[256,512]{1,0:T(8,128)(2,1)}, f32[512,256]{1,0:T(8,128)S(1)}, f32[512,256]{1,0:T(8,128)S(1)}) custom-call(bf16[3,512,256]{2,1,0:T(8,128)(2,1)S(1)} %copy-done, bf16[3,2,256]{2,1,0:T(2,128)(2,1)S(1)} %collective-permute-done.halo_ref, f32[3,3,256]{2,1,0:T(4,128)S(1)} %copy-done.1, f32[3,256]{1,0:T(4,128)S(1)} %copy-done.2, ...), custom_call_target="tpu_custom_call" | custom-call | flops 2621440 | bytes 2097152 | tf_op jit(solution)/shard_map/short_conv/pallas_call | solution.py:161
  29.7 26.1 %all-to-all-done.1.recv_ref = bf16[512,8,128]{2,1,0:T(8,128)(2,1)S(1)} async-done(((bf16[512,8,128]{2,1,0:T(8,128)(2,1)}), bf16[512,8,128]{2,1,0:T(8,128)(2,1)S(1)}, u32[]{:S(2)}, u32[]{:S(2)}) %all-to-all-start.1) | async-done | bytes 1048608 | tf_op jit(solution)/shard_map/all_to_all | solution.py:343
  55.8 0.0 copy-start.5
  55.8 5.8 %all-to-all-start = ((bf16[32,8,512]{2,1,0:T(8,128)(2,1)}), bf16[32,8,512]{2,1,0:T(8,128)(2,1)S(1)}, u32[]{:S(2)}, u32[]{:S(2)}) async-start(bf16[32,8,512]{2,1,0:T(8,128)(2,1)} %bitcast.1), calls=%async_computation | async-start | bytes 524288 | tf_op jit(solution)/shard_map/all_to_all | solution.py:343
  61.6 0.0 copy-done.5
  61.6 0.0 copy-start.4
  61.7 3.2 %arrange_filter.1.refs_4_ = bf16[544,512]{1,0:T(8,128)(2,1)S(1)} custom-call(bf16[512,8,128]{2,1,0:T(8,128)(2,1)S(1)} %all-to-all-done.1.recv_ref, bf16[160,128]{1,0:T(8,128)(2,1)S(1)} %copy-done.5), custom_call_target="tpu_custom_call" | custom-call | flops 536870912 | bytes 3145728 | tf_op jit(solution)/shard_map/arrange_filter/pallas_call | solution.py:208
  64.8 0.0 copy-start.6
  64.8 0.8 copy-done.6
  65.6 8.4 %all-to-all-done = bf16[32,8,512]{2,1,0:T(8,128)(2,1)S(1)} async-done(((bf16[32,8,512]{2,1,0:T(8,128)(2,1)}), bf16[32,8,512]{2,1,0:T(8,128)(2,1)S(1)}, u32[]{:S(2)}, u32[]{:S(2)}) %all-to-all-start) | async-done | bytes 262176 | tf_op jit(solution)/shard_map/all_to_all | solution.py:343
  74.0 0.0 copy-done.4
  74.0 3.2 %transform.1 = bf16[256,512]{1,0:T(8,128)(2,1)S(1)} custom-call(bf16[256,512]{1,0:T(8,128)(2,1)S(1)} %bitcast.7, bf16[544,256]{1,0:T(8,128)(2,1)} %constant.11.clone.refs_1_, f32[2,96,512]{2,1,0:T(8,128)} %constant.12.clone.refs_2_, bf16[512,256]{1,0:T(8,128)(2,1)S(1)} %copy-done.4, bf16[544,512]{1,0:T(8,128)(2,1)} %copy-done.6, ...), custom_call_target="tpu_custom_call" | custom-call | flops 855638016 | bytes 6291456 | tf_op jit(solution)/shard_map/transform/pallas_call | solution.py:306
  77.2 15.6 %all_to_all.15 = bf16[32,8,512]{2,1,0:T(8,128)(2,1)S(1)} all-to-all(bf16[32,8,512]{2,1,0:T(8,128)(2,1)S(1)} %bitcast.8), channel_id=1, replica_groups=mesh['seq'=32,'chan'=16] {'seq'}, dimensions={0} | all-to-all | bytes 524288 | tf_op jit(solution)/shard_map/all_to_all | solution.py:343
  92.8 0.8 finish.1
  (1 shorter events, 0.0 us)
Async XLA Ops:
  2.2 21.1 %copy-start = (bf16[3,512,256]{2,1,0:T(8,128)(2,1)S(1)}, bf16[3,512,256]{2,1,0:T(8,128)(2,1)}, u32[]{:S(2)}) copy-start(bf16[3,512,256]{2,1,0:T(8,128)(2,1)} %streams_ref.1) | copy-start | bytes 2359300
  2.3 25.9 %copy-start.1 = (f32[3,3,256]{2,1,0:T(4,128)S(1)}, f32[3,3,256]{2,1,0:T(4,128)}, u32[]{:S(2)}) copy-start(f32[3,3,256]{2,1,0:T(4,128)} %weight_ref.1) | copy-start | bytes 27652
  2.3 53.6 %all-to-all-start.1 = ((bf16[512,8,128]{2,1,0:T(8,128)(2,1)}), bf16[512,8,128]{2,1,0:T(8,128)(2,1)S(1)}, u32[]{:S(2)}, u32[]{:S(2)}) async-start(bf16[512,8,128]{2,1,0:T(8,128)(2,1)} %bitcast.10), calls=%async_computation.1 | async-start | bytes 2097152 | tf_op jit(solution)/shard_map/all_to_all | solution.py:343
  23.4 4.7 %copy-start.2 = (f32[3,256]{1,0:T(4,128)S(1)}, f32[3,256]{1,0:T(4,128)}, u32[]{:S(2)}) copy-start(f32[3,256]{1,0:T(4,128)} %bias_ref.1) | copy-start | bytes 9220
  23.4 4.7 %copy-start.3 = (f32[256]{0:T(256)S(1)}, f32[256]{0:T(256)}, u32[]{:S(2)}) copy-start(f32[256]{0:T(256)} %param.14) | copy-start | bytes 3076
  23.4 4.7 %collective-permute-start = (bf16[3,2,256]{2,1,0:T(2,128)(2,1)S(1)}, bf16[3,2,256]{2,1,0:T(2,128)(2,1)S(1)}, u32[]{:S(2)}, u32[]{:S(2)}) collective-permute-start(bf16[3,2,256]{2,1,0:T(2,128)(2,1)S(1)} %slice.3), channel_id=1, source_target_pairs={{0,16},{16,32},{32,48},{48,64},{64,80},{80,96},{96,112},{112,128},... | collective-permute-start | bytes 9224 | tf_op jit(solution)/shard_map/ppermute | solution.py:357
  55.8 5.8 %copy-start.5 = (bf16[160,128]{1,0:T(8,128)(2,1)S(1)}, bf16[160,128]{1,0:T(8,128)(2,1)}, u32[]{:S(2)}) copy-start(bf16[160,128]{1,0:T(8,128)(2,1)} %constant.10.clone.fold_ref) | copy-start | bytes 122884
  55.8 18.2 %all-to-all-start = ((bf16[32,8,512]{2,1,0:T(8,128)(2,1)}), bf16[32,8,512]{2,1,0:T(8,128)(2,1)S(1)}, u32[]{:S(2)}, u32[]{:S(2)}) async-start(bf16[32,8,512]{2,1,0:T(8,128)(2,1)} %bitcast.1), calls=%async_computation | async-start | bytes 524288 | tf_op jit(solution)/shard_map/all_to_all | solution.py:343
  61.6 12.3 %copy-start.4 = (bf16[512,256]{1,0:T(8,128)(2,1)S(1)}, bf16[512,256]{1,0:T(8,128)(2,1)}, u32[]{:S(2)}) copy-start(bf16[512,256]{1,0:T(8,128)(2,1)} %constant.13.clone.refs_3_) | copy-start | bytes 786436
  64.8 0.8 copy-start.6

commit v4 on v3

--- a/solution.py
+++ b/solution.py
@@ -11,7 +11,7 @@
 F32 = jnp.float32
 BF16 = jnp.bfloat16
 VMEM_LIMIT = 20 * 1024 * 1024
-VMEM_WHOLE = 53 * 1024 * 1024
+VMEM_WHOLE = 52 * 1024 * 1024
 
 
 def dot_t(lhs, rhs):
@@ -221,27 +221,19 @@
 
 
 def transform_kernel(plan, *refs):
-    count = 6
-    sources, y_ref, held = refs[:count], refs[count], refs[count + 1 : 2 * count + 1]
-    left_ref, b_ref, sems = refs[2 * count + 1 :]
+    u_ref, first_ref, tw_ref, filt_ref, *sources = refs[:6]
+    y_ref, big_ref, last_ref, left_ref, b_ref, sems = refs[6:]
     fetches = [
-        pltpu.make_async_copy(
-            s.at[:, : h.shape[1]] if len(h.shape) == 3 else s, h, sems.at[j]
-        )
-        for j, (s, h) in enumerate(zip(sources, held))
+        pltpu.make_async_copy(s.at[: h.shape[0]], h, sems.at[j])
+        for j, (s, h) in enumerate(zip(sources, (big_ref, last_ref)))
     ]
     for fetch in fetches:
         fetch.start()
-    u_ref, first_ref, tw_ref, big_ref, filt_ref, last_ref = held
     seq, rows, base, span = plan.seq, plan.rows, plan.base, plan.span
-    fetches[0].wait()
-    fetches[1].wait()
     u = u_ref[...]
     stages = [
         dot(first_ref[2 * g * rows : 2 * (g + 1) * rows, :], u) for g in range(plan.groups)
     ]
-    fetches[2].wait()
-
     half = span // 2
 
     def turn(re, im):
@@ -275,8 +267,7 @@
         ]
 
     turned = [turn(stage[:rows], stage[rows:]) for stage in stages]
-    fetches[3].wait()
-    fetches[4].wait()
+    fetches[0].wait()
     for g in range(plan.groups):
         lo, mid, hi = (2 * g) * rows, (2 * g + 1) * rows, (2 * g + 2) * rows
         re, im = turned[g]
@@ -294,7 +285,7 @@
         )
         b_ref[lo:mid, :] = br.astype(BF16)
         b_ref[mid:hi, :] = bi.astype(BF16)
-    fetches[5].wait()
+    fetches[1].wait()
     y_ref[...] = dot(last_ref[...], b_ref[...]).astype(BF16)
 
 
@@ -302,24 +293,23 @@
     rows, span = plan.groups * plan.rows, plan.span
     macs = 2 * (2 * rows * u.shape[0] * span + 2 * span * span * rows)
     first, tw, big, last = tables
-    sources = (u, first, tw, big, filt, last)
+    whole = pl.BlockSpec(memory_space=pltpu.VMEM)
     return pl.pallas_call(
         functools.partial(transform_kernel, plan),
-        in_specs=[pl.BlockSpec(memory_space=pl.ANY)] * len(sources),
-        out_specs=pl.BlockSpec(memory_space=pltpu.VMEM),
+        in_specs=[whole] * 4 + [pl.BlockSpec(memory_space=pl.ANY)] * 2,
+        out_specs=whole,
         out_shape=jax.ShapeDtypeStruct(u.shape, BF16),
-        scratch_shapes=[pltpu.VMEM(s.shape, s.dtype) for s in (u, first)]
-        + [pltpu.VMEM((2, plan.seq + plan.spare + 8, span), F32)]
-        + [pltpu.VMEM(s.shape, s.dtype) for s in (big, filt, last)]
-        + [
+        scratch_shapes=[
+            pltpu.VMEM((span, span // 2), BF16),
+            pltpu.VMEM((u.shape[0], last.shape[1]), BF16),
             pltpu.VMEM((4 * plan.rows, span), BF16),
             pltpu.VMEM((2 * rows, span), BF16),
-            pltpu.SemaphoreType.DMA((len(sources),)),
+            pltpu.SemaphoreType.DMA((2,)),
         ],
         cost_estimate=pl.CostEstimate(flops=2 * macs, bytes_accessed=6 * 1024 * 1024, transcendentals=0),
         compiler_params=pltpu.CompilerParams(vmem_limit_bytes=VMEM_WHOLE),
         name="transform",
-    )(*sources)
+    )(u, first, tw, filt, big, last)
 
 
 def final_kernel(y_ref, direct_ref, gate_ref, out_ref):
@@ -369,9 +359,9 @@
     fold = jnp.asarray(plan.fold_table(), BF16)
     tables = (
         jnp.asarray(plan.first_table(), BF16),
-        jnp.asarray(np.pad(plan.twiddle(), ((0, 0), (0, 40), (0, 0))), F32),
-        jnp.asarray(plan.big_table(), BF16),
-        jnp.asarray(plan.last_table(), BF16),
+        jnp.asarray(plan.twiddle(), F32),
+        jnp.asarray(np.pad(plan.big_table(), ((0, 2048), (0, 0))), BF16),
+        jnp.asarray(np.pad(plan.last_table(), ((0, 1024), (0, 0))), BF16),
     )
     placed = (
         P(None, "seq", "chan"),

time: 94 us -> 93.4 us (level)
  Pallas kernels: 11 us -> 9.89 us
  transfers between devices with their start and end apart: 3 -> 3, of which waited for: 3 -> 3; matrix products, arithmetic and copies ran while one was open for 0% -> 0% of each run, Pallas kernels for 5% -> 4%
where the time goes in v4:
time: 93.4 us; the launch traced here: 93.1 us
  waiting for transfers between devices  36.6 us (39%)
  starting transfers between devices  30.2 us (32%)
  blocking collectives  15.6 us (17%)
  Pallas kernels  9.89 us (11%)
    all_to_all x2, waiting for transfers between devices, exchange(): return lax.all_to_all(values, axes, split_axis=0, concat_axis=0, tiled=True)  35.3 us
    all_to_all x2, starting transfers between devices, exchange(): return lax.all_to_all(values, axes, split_axis=0, concat_axis=0, tiled=True)  26.8 us
    all_to_all x1, blocking collectives, exchange(): return lax.all_to_all(values, axes, split_axis=0, concat_axis=0, tiled=True)  15.6 us
    ppermute x1, starting transfers between devices, on_device(): halo = lax.ppermute(streams[:, length - 2:, :], 'seq', route)  3.37 us
    pallas_call x1, Pallas kernels, arrange_filter(): pl.pallas_call(functools.partial(filter_kernel, plan), out_shape=jax.Shap...  3.16 us
    pallas_call x1, Pallas kernels, transform(): pl.pallas_call(functools.partial(transform_kernel, plan), in_specs=[whole...  2.75 us
    pallas_call x1, Pallas kernels, transpose_spectrum(): pl.pallas_call(spectrum_kernel, in_specs=[pl.BlockSpec(memory_space=pl.AN...  2.3 us
  transfers between devices with their start and end apart: 3, of which 3 were waited for; matrix products, arithmetic and copies ran while one was open for 0% of the time, Pallas kernels for 4%

profile of v4, /device:TPU:8, one launch (start us, length us, event | category | flops | bytes accessed | tf_op | source)
XLA Modules:
  0.0 93.1 jit_solution(17410275450407738440)
XLA Ops:
  0.0 0.0 copy-start
  0.0 0.0 copy-start.6
  0.0 0.0 copy-start.5
  0.0 0.0 copy-start.4
  0.0 2.3 %transpose_spectrum.1 = bf16[4096,128]{1,0:T(8,128)(2,1)} custom-call(bf16[2,2,32,4096]{3,2,1,0:T(8,128)(2,1)} %spec_ref.1), custom_call_target="tpu_custom_call" | custom-call | flops 524288 | bytes 2097152 | tf_op jit(solution)/shard_map/transpose_spectrum/pallas_call | solution.py:120
  2.3 0.0 copy-start.7
  2.3 21.1 %all-to-all-start.1 = ((bf16[512,8,128]{2,1,0:T(8,128)(2,1)}), bf16[512,8,128]{2,1,0:T(8,128)(2,1)S(1)}, u32[]{:S(2)}, u32[]{:S(2)}) async-start(bf16[512,8,128]{2,1,0:T(8,128)(2,1)} %bitcast.3), calls=%async_computation.1 | async-start | bytes 2097152 | tf_op jit(solution)/shard_map/all_to_all | solution.py:333
  23.5 0.0 copy-done
  23.5 3.4 %collective-permute-start = (bf16[3,2,256]{2,1,0:T(2,128)(2,1)S(1)}, bf16[3,2,256]{2,1,0:T(2,128)(2,1)S(1)}, u32[]{:S(2)}, u32[]{:S(2)}) collective-permute-start(bf16[3,2,256]{2,1,0:T(2,128)(2,1)S(1)} %slice.3), channel_id=1, source_target_pairs={{0,16},{16,32},{32,48},{48,64},{64,80},{80,96},{96,112},{112,128},... | collective-permute-start | bytes 9224 | tf_op jit(solution)/shard_map/ppermute | solution.py:347
  26.9 1.3 %collective-permute-done.halo_ref = bf16[3,2,256]{2,1,0:T(2,128)(2,1)S(1)} collective-permute-done((bf16[3,2,256]{2,1,0:T(2,128)(2,1)S(1)}, bf16[3,2,256]{2,1,0:T(2,128)(2,1)S(1)}, u32[]{:S(2)}, u32[]{:S(2)}) %collective-permute-start) | collective-permute-done | bytes 3104 | tf_op jit(solution)/shard_map/ppermute | solution.py:347
  28.2 0.0 copy-done.6
  28.2 0.0 copy-done.5
  28.2 0.0 copy-done.4
  28.2 0.0 copy-start.1
  28.2 0.8 short_conv.1
  29.0 0.0 copy-start.2
  29.0 0.7 copy-done.2
  29.7 0.0 copy-start.3
  29.7 26.2 %all-to-all-done.1.recv_ref = bf16[512,8,128]{2,1,0:T(8,128)(2,1)S(1)} async-done(((bf16[512,8,128]{2,1,0:T(8,128)(2,1)}), bf16[512,8,128]{2,1,0:T(8,128)(2,1)S(1)}, u32[]{:S(2)}, u32[]{:S(2)}) %all-to-all-start.1) | async-done | bytes 1048608 | tf_op jit(solution)/shard_map/all_to_all | solution.py:333
  55.9 5.7 %all-to-all-start = ((bf16[32,8,512]{2,1,0:T(8,128)(2,1)}), bf16[32,8,512]{2,1,0:T(8,128)(2,1)S(1)}, u32[]{:S(2)}, u32[]{:S(2)}) async-start(bf16[32,8,512]{2,1,0:T(8,128)(2,1)} %bitcast.9), calls=%async_computation | async-start | bytes 524288 | tf_op jit(solution)/shard_map/all_to_all | solution.py:333
  61.6 0.0 copy-done.7
  61.6 3.2 %arrange_filter.1.refs_3_ = bf16[544,512]{1,0:T(8,128)(2,1)S(1)} custom-call(bf16[512,8,128]{2,1,0:T(8,128)(2,1)S(1)} %all-to-all-done.1.recv_ref, bf16[160,128]{1,0:T(8,128)(2,1)S(1)} %copy-done.7), custom_call_target="tpu_custom_call" | custom-call | flops 536870912 | bytes 3145728 | tf_op jit(solution)/shard_map/arrange_filter/pallas_call | solution.py:208
  64.8 9.2 %all-to-all-done = bf16[32,8,512]{2,1,0:T(8,128)(2,1)S(1)} async-done(((bf16[32,8,512]{2,1,0:T(8,128)(2,1)}), bf16[32,8,512]{2,1,0:T(8,128)(2,1)S(1)}, u32[]{:S(2)}, u32[]{:S(2)}) %all-to-all-start) | async-done | bytes 262176 | tf_op jit(solution)/shard_map/all_to_all | solution.py:333
  73.9 0.0 copy-done.1
  73.9 0.0 copy-done.3
  73.9 2.7 %transform.1 = bf16[256,512]{1,0:T(8,128)(2,1)S(1)} custom-call(bf16[256,512]{1,0:T(8,128)(2,1)S(1)} %bitcast.6, bf16[544,256]{1,0:T(8,128)(2,1)S(1)} %copy-done.1, f32[2,56,512]{2,1,0:T(8,128)S(1)} %copy-done.3, bf16[544,512]{1,0:T(8,128)(2,1)S(1)} %arrange_filter.1.refs_3_, bf16[2560,256]{1,0:T(8,128)(2,1)} %constant.13.clone.refs_4_, ...), custom_call_target="tpu_custom_call" | custom-call | flops 855638016 | bytes 6291456 | tf_op jit(solution)/shard_map/transform/pallas_call | solution.py:297
  76.7 15.6 %all_to_all.15 = bf16[32,8,512]{2,1,0:T(8,128)(2,1)S(1)} all-to-all(bf16[32,8,512]{2,1,0:T(8,128)(2,1)S(1)} %bitcast.7), channel_id=1, replica_groups=mesh['seq'=32,'chan'=16] {'seq'}, dimensions={0} | all-to-all | bytes 524288 | tf_op jit(solution)/shard_map/all_to_all | solution.py:333
  92.2 0.8 finish.1
  (1 shorter events, 0.0 us)
Async XLA Ops:
  0.0 23.5 %copy-start = (bf16[3,512,256]{2,1,0:T(8,128)(2,1)S(1)}, bf16[3,512,256]{2,1,0:T(8,128)(2,1)}, u32[]{:S(2)}) copy-start(bf16[3,512,256]{2,1,0:T(8,128)(2,1)} %streams_ref.1) | copy-start | bytes 2359300
  0.0 28.2 %copy-start.6 = (f32[256]{0:T(256)S(1)}, f32[256]{0:T(256)}, u32[]{:S(2)}) copy-start(f32[256]{0:T(256)} %param.14) | copy-start | bytes 3076
  0.0 28.2 %copy-start.5 = (f32[3,256]{1,0:T(4,128)S(1)}, f32[3,256]{1,0:T(4,128)}, u32[]{:S(2)}) copy-start(f32[3,256]{1,0:T(4,128)} %bias_ref.1) | copy-start | bytes 9220
  0.0 28.2 %copy-start.4 = (f32[3,3,256]{2,1,0:T(4,128)S(1)}, f32[3,3,256]{2,1,0:T(4,128)}, u32[]{:S(2)}) copy-start(f32[3,3,256]{2,1,0:T(4,128)} %weight_ref.1) | copy-start | bytes 27652
  2.3 59.3 %copy-start.7 = (bf16[160,128]{1,0:T(8,128)(2,1)S(1)}, bf16[160,128]{1,0:T(8,128)(2,1)}, u32[]{:S(2)}) copy-start(bf16[160,128]{1,0:T(8,128)(2,1)} %constant.10.clone.fold_ref) | copy-start | bytes 122884
  2.3 53.6 %all-to-all-start.1 = ((bf16[512,8,128]{2,1,0:T(8,128)(2,1)}), bf16[512,8,128]{2,1,0:T(8,128)(2,1)S(1)}, u32[]{:S(2)}, u32[]{:S(2)}) async-start(bf16[512,8,128]{2,1,0:T(8,128)(2,1)} %bitcast.3), calls=%async_computation.1 | async-start | bytes 2097152 | tf_op jit(solution)/shard_map/all_to_all | solution.py:333
  23.5 4.7 %collective-permute-start = (bf16[3,2,256]{2,1,0:T(2,128)(2,1)S(1)}, bf16[3,2,256]{2,1,0:T(2,128)(2,1)S(1)}, u32[]{:S(2)}, u32[]{:S(2)}) collective-permute-start(bf16[3,2,256]{2,1,0:T(2,128)(2,1)S(1)} %slice.3), channel_id=1, source_target_pairs={{0,16},{16,32},{32,48},{48,64},{64,80},{80,96},{96,112},{112,128},... | collective-permute-start | bytes 9224 | tf_op jit(solution)/shard_map/ppermute | solution.py:347
  28.2 45.8 %copy-start.1 = (bf16[544,256]{1,0:T(8,128)(2,1)S(1)}, bf16[544,256]{1,0:T(8,128)(2,1)}, u32[]{:S(2)}) copy-start(bf16[544,256]{1,0:T(8,128)(2,1)} %constant.11.clone.refs_1_) | copy-start | bytes 835588
  29.0 0.7 copy-start.2
  29.7 44.2 %copy-start.3 = (f32[2,56,512]{2,1,0:T(8,128)S(1)}, f32[2,56,512]{2,1,0:T(8,128)}, u32[]{:S(2)}) copy-start(f32[2,56,512]{2,1,0:T(8,128)} %constant.12.clone.refs_2_) | copy-start | bytes 688132
  55.9 18.0 %all-to-all-start = ((bf16[32,8,512]{2,1,0:T(8,128)(2,1)}), bf16[32,8,512]{2,1,0:T(8,128)(2,1)S(1)}, u32[]{:S(2)}, u32[]{:S(2)}) async-start(bf16[32,8,512]{2,1,0:T(8,128)(2,1)} %bitcast.9), calls=%async_computation | async-start | bytes 524288 | tf_op jit(solution)/shard_map/all_to_all | solution.py:333

commit v5 on v4

--- a/solution.py
+++ b/solution.py
@@ -267,12 +267,13 @@
         ]
 
     turned = [turn(stage[:rows], stage[rows:]) for stage in stages]
-    fetches[0].wait()
     for g in range(plan.groups):
         lo, mid, hi = (2 * g) * rows, (2 * g + 1) * rows, (2 * g + 2) * rows
         re, im = turned[g]
         even = (re[:, :half] + re[:, half:], im[:, :half] + im[:, half:])
         odd = step(re[:, :half] - re[:, half:], im[:, :half] - im[:, half:])
+        if g == 0:
+            fetches[0].wait()
         weighted = []
         for j, (xr, xi) in enumerate(multiply([even, odd])):
             hr = filt_ref[lo:mid, j * half : (j + 1) * half].astype(F32)

time: 93.4 us -> 93.4 us (level)
  no operation moved by 1% of the time
where the time goes in v5:
time: 93.4 us; the launch traced here: 93.1 us
  waiting for transfers between devices  36.6 us (39%)
  starting transfers between devices  30.2 us (32%)
  blocking collectives  15.6 us (17%)
  Pallas kernels  9.88 us (11%)
    all_to_all x2, waiting for transfers between devices, exchange(): return lax.all_to_all(values, axes, split_axis=0, concat_axis=0, tiled=True)  35.3 us
    all_to_all x2, starting transfers between devices, exchange(): return lax.all_to_all(values, axes, split_axis=0, concat_axis=0, tiled=True)  26.8 us
    all_to_all x1, blocking collectives, exchange(): return lax.all_to_all(values, axes, split_axis=0, concat_axis=0, tiled=True)  15.6 us
    ppermute x1, starting transfers between devices, on_device(): halo = lax.ppermute(streams[:, length - 2:, :], 'seq', route)  3.37 us
    pallas_call x1, Pallas kernels, arrange_filter(): pl.pallas_call(functools.partial(filter_kernel, plan), out_shape=jax.Shap...  3.16 us
    pallas_call x1, Pallas kernels, transform(): pl.pallas_call(functools.partial(transform_kernel, plan), in_specs=[whole...  2.74 us
    pallas_call x1, Pallas kernels, transpose_spectrum(): pl.pallas_call(spectrum_kernel, in_specs=[pl.BlockSpec(memory_space=pl.AN...  2.3 us
  transfers between devices with their start and end apart: 3, of which 3 were waited for; matrix products, arithmetic and copies ran while one was open for 0% of the time, Pallas kernels for 4%

profile of v5, /device:TPU:8, one launch (start us, length us, event | category | flops | bytes accessed | tf_op | source)
XLA Modules:
  0.0 93.1 jit_solution(12798549938594291597)
XLA Ops:
  0.0 0.0 copy-start
  0.0 0.0 copy-start.6
  0.0 0.0 copy-start.5
  0.0 0.0 copy-start.4
  0.0 2.3 %transpose_spectrum.1 = bf16[4096,128]{1,0:T(8,128)(2,1)} custom-call(bf16[2,2,32,4096]{3,2,1,0:T(8,128)(2,1)} %spec_ref.1), custom_call_target="tpu_custom_call" | custom-call | flops 524288 | bytes 2097152 | tf_op jit(solution)/shard_map/transpose_spectrum/pallas_call | solution.py:120
  2.3 0.0 copy-start.7
  2.3 21.1 %all-to-all-start.1 = ((bf16[512,8,128]{2,1,0:T(8,128)(2,1)}), bf16[512,8,128]{2,1,0:T(8,128)(2,1)S(1)}, u32[]{:S(2)}, u32[]{:S(2)}) async-start(bf16[512,8,128]{2,1,0:T(8,128)(2,1)} %bitcast.3), calls=%async_computation.1 | async-start | bytes 2097152 | tf_op jit(solution)/shard_map/all_to_all | solution.py:334
  23.5 0.0 copy-done
  23.5 3.4 %collective-permute-start = (bf16[3,2,256]{2,1,0:T(2,128)(2,1)S(1)}, bf16[3,2,256]{2,1,0:T(2,128)(2,1)S(1)}, u32[]{:S(2)}, u32[]{:S(2)}) collective-permute-start(bf16[3,2,256]{2,1,0:T(2,128)(2,1)S(1)} %slice.3), channel_id=1, source_target_pairs={{0,16},{16,32},{32,48},{48,64},{64,80},{80,96},{96,112},{112,128},... | collective-permute-start | bytes 9224 | tf_op jit(solution)/shard_map/ppermute | solution.py:348
  26.9 1.3 %collective-permute-done.halo_ref = bf16[3,2,256]{2,1,0:T(2,128)(2,1)S(1)} collective-permute-done((bf16[3,2,256]{2,1,0:T(2,128)(2,1)S(1)}, bf16[3,2,256]{2,1,0:T(2,128)(2,1)S(1)}, u32[]{:S(2)}, u32[]{:S(2)}) %collective-permute-start) | collective-permute-done | bytes 3104 | tf_op jit(solution)/shard_map/ppermute | solution.py:348
  28.2 0.0 copy-done.6
  28.2 0.0 copy-done.5
  28.2 0.0 copy-done.4
  28.2 0.0 copy-start.1
  28.2 0.8 short_conv.1
  29.0 0.0 copy-start.2
  29.0 0.7 copy-done.2
  29.7 0.0 copy-start.3
  29.7 26.2 %all-to-all-done.1.recv_ref = bf16[512,8,128]{2,1,0:T(8,128)(2,1)S(1)} async-done(((bf16[512,8,128]{2,1,0:T(8,128)(2,1)}), bf16[512,8,128]{2,1,0:T(8,128)(2,1)S(1)}, u32[]{:S(2)}, u32[]{:S(2)}) %all-to-all-start.1) | async-done | bytes 1048608 | tf_op jit(solution)/shard_map/all_to_all | solution.py:334
  55.9 5.7 %all-to-all-start = ((bf16[32,8,512]{2,1,0:T(8,128)(2,1)}), bf16[32,8,512]{2,1,0:T(8,128)(2,1)S(1)}, u32[]{:S(2)}, u32[]{:S(2)}) async-start(bf16[32,8,512]{2,1,0:T(8,128)(2,1)} %bitcast.9), calls=%async_computation | async-start | bytes 524288 | tf_op jit(solution)/shard_map/all_to_all | solution.py:334
  61.6 0.0 copy-done.7
  61.6 3.2 %arrange_filter.1.refs_3_ = bf16[544,512]{1,0:T(8,128)(2,1)S(1)} custom-call(bf16[512,8,128]{2,1,0:T(8,128)(2,1)S(1)} %all-to-all-done.1.recv_ref, bf16[160,128]{1,0:T(8,128)(2,1)S(1)} %copy-done.7), custom_call_target="tpu_custom_call" | custom-call | flops 536870912 | bytes 3145728 | tf_op jit(solution)/shard_map/arrange_filter/pallas_call | solution.py:208
  64.8 9.2 %all-to-all-done = bf16[32,8,512]{2,1,0:T(8,128)(2,1)S(1)} async-done(((bf16[32,8,512]{2,1,0:T(8,128)(2,1)}), bf16[32,8,512]{2,1,0:T(8,128)(2,1)S(1)}, u32[]{:S(2)}, u32[]{:S(2)}) %all-to-all-start) | async-done | bytes 262176 | tf_op jit(solution)/shard_map/all_to_all | solution.py:334
  73.9 0.0 copy-done.1
  73.9 0.0 copy-done.3
  73.9 2.7 %transform.1 = bf16[256,512]{1,0:T(8,128)(2,1)S(1)} custom-call(bf16[256,512]{1,0:T(8,128)(2,1)S(1)} %bitcast.6, bf16[544,256]{1,0:T(8,128)(2,1)S(1)} %copy-done.1, f32[2,56,512]{2,1,0:T(8,128)S(1)} %copy-done.3, bf16[544,512]{1,0:T(8,128)(2,1)S(1)} %arrange_filter.1.refs_3_, bf16[2560,256]{1,0:T(8,128)(2,1)} %constant.13.clone.refs_4_, ...), custom_call_target="tpu_custom_call" | custom-call | flops 855638016 | bytes 6291456 | tf_op jit(solution)/shard_map/transform/pallas_call | solution.py:298
  76.7 15.6 %all_to_all.15 = bf16[32,8,512]{2,1,0:T(8,128)(2,1)S(1)} all-to-all(bf16[32,8,512]{2,1,0:T(8,128)(2,1)S(1)} %bitcast.7), channel_id=1, replica_groups=mesh['seq'=32,'chan'=16] {'seq'}, dimensions={0} | all-to-all | bytes 524288 | tf_op jit(solution)/shard_map/all_to_all | solution.py:334
  92.2 0.8 finish.1
  (1 shorter events, 0.0 us)
Async XLA Ops:
  0.0 23.5 %copy-start = (bf16[3,512,256]{2,1,0:T(8,128)(2,1)S(1)}, bf16[3,512,256]{2,1,0:T(8,128)(2,1)}, u32[]{:S(2)}) copy-start(bf16[3,512,256]{2,1,0:T(8,128)(2,1)} %streams_ref.1) | copy-start | bytes 2359300
  0.0 28.2 %copy-start.6 = (f32[256]{0:T(256)S(1)}, f32[256]{0:T(256)}, u32[]{:S(2)}) copy-start(f32[256]{0:T(256)} %param.14) | copy-start | bytes 3076
  0.0 28.2 %copy-start.5 = (f32[3,256]{1,0:T(4,128)S(1)}, f32[3,256]{1,0:T(4,128)}, u32[]{:S(2)}) copy-start(f32[3,256]{1,0:T(4,128)} %bias_ref.1) | copy-start | bytes 9220
  0.0 28.2 %copy-start.4 = (f32[3,3,256]{2,1,0:T(4,128)S(1)}, f32[3,3,256]{2,1,0:T(4,128)}, u32[]{:S(2)}) copy-start(f32[3,3,256]{2,1,0:T(4,128)} %weight_ref.1) | copy-start | bytes 27652
  2.3 59.3 %copy-start.7 = (bf16[160,128]{1,0:T(8,128)(2,1)S(1)}, bf16[160,128]{1,0:T(8,128)(2,1)}, u32[]{:S(2)}) copy-start(bf16[160,128]{1,0:T(8,128)(2,1)} %constant.10.clone.fold_ref) | copy-start | bytes 122884
  2.3 53.6 %all-to-all-start.1 = ((bf16[512,8,128]{2,1,0:T(8,128)(2,1)}), bf16[512,8,128]{2,1,0:T(8,128)(2,1)S(1)}, u32[]{:S(2)}, u32[]{:S(2)}) async-start(bf16[512,8,128]{2,1,0:T(8,128)(2,1)} %bitcast.3), calls=%async_computation.1 | async-start | bytes 2097152 | tf_op jit(solution)/shard_map/all_to_all | solution.py:334
  23.5 4.7 %collective-permute-start = (bf16[3,2,256]{2,1,0:T(2,128)(2,1)S(1)}, bf16[3,2,256]{2,1,0:T(2,128)(2,1)S(1)}, u32[]{:S(2)}, u32[]{:S(2)}) collective-permute-start(bf16[3,2,256]{2,1,0:T(2,128)(2,1)S(1)} %slice.3), channel_id=1, source_target_pairs={{0,16},{16,32},{32,48},{48,64},{64,80},{80,96},{96,112},{112,128},... | collective-permute-start | bytes 9224 | tf_op jit(solution)/shard_map/ppermute | solution.py:348
  28.2 45.8 %copy-start.1 = (bf16[544,256]{1,0:T(8,128)(2,1)S(1)}, bf16[544,256]{1,0:T(8,128)(2,1)}, u32[]{:S(2)}) copy-start(bf16[544,256]{1,0:T(8,128)(2,1)} %constant.11.clone.refs_1_) | copy-start | bytes 835588
  29.0 0.7 copy-start.2
  29.7 44.2 %copy-start.3 = (f32[2,56,512]{2,1,0:T(8,128)S(1)}, f32[2,56,512]{2,1,0:T(8,128)}, u32[]{:S(2)}) copy-start(f32[2,56,512]{2,1,0:T(8,128)} %constant.12.clone.refs_2_) | copy-start | bytes 688132
  55.9 18.0 %all-to-all-start = ((bf16[32,8,512]{2,1,0:T(8,128)(2,1)}), bf16[32,8,512]{2,1,0:T(8,128)(2,1)S(1)}, u32[]{:S(2)}, u32[]{:S(2)}) async-start(bf16[32,8,512]{2,1,0:T(8,128)(2,1)} %bitcast.9), calls=%async_computation | async-start | bytes 524288 | tf_op jit(solution)/shard_map/all_to_all | solution.py:334
